TPU v7x, 256 devices: a whole 4x4x8 slice. The times are simulated.
256 devices in a mesh: ctx: 32 (over z, x), head: 8 (over y, core).
Axes of the slice: x: 4, y: 4, z: 8, core: 2. Of those that a mesh axis runs over, the one named last changes fastest.
Arguments:
- query: bfloat16 [8192, 2048], P('ctx', 'head'), may hold values from -6.5 to 6.5
- key: bfloat16 [8192, 2048], P('ctx', 'head'), may hold values from -6.5 to 6.5
- value: bfloat16 [8192, 2048], P('ctx', 'head'), may hold values from -6 to 6
- householder: bfloat16 [8192, 2048], P('ctx', 'head'), may hold values from -4 to 4, as said below
- cotangent: bfloat16 [8192, 2048], P('ctx', 'head'), may hold values from -6 to 6
- w_query: bfloat16 [4096, 2048], P(None, 'head'), may hold values from -0.09375 to 0.09375
- w_key: bfloat16 [4096, 2048], P(None, 'head'), may hold values from -0.09375 to 0.09375
- w_value: bfloat16 [4096, 2048], P(None, 'head'), may hold values from -0.09375 to 0.09375
Outputs:
- input_grad: float32 [8192, 4096], P('ctx', 'head')
Inputs may be any that keep to these rules, and one draw needn't show every extreme that they name: `householder`: no token has a head whose vector is zero.
All inputs are finite; a program needn't handle non-finite values.
Results may differ from a plain program's by a relative error of at most 0.01705.
Values may be sent and summed in bfloat16 or wider, within the bound.
A program may use at most 128 MiB of HBM per device.

v0:
```python
import jax
import jax.numpy as jnp
from jax import lax
from jax.sharding import PartitionSpec as P

HEAD_DIM = 128


precise_setting = lax.Precision.HIGHEST


def prefix(value, axis, join, neutral):
    count, mine = (lax.axis_size(axis), lax.axis_index(axis))
    pieces = lax.all_gather(value, axis)
    running = jnp.full_like(value, 0) + jnp.asarray(neutral, value.dtype)

    def turn(position, running):
        longer = join(running, pieces[position])
        return jnp.where(position < mine, longer, running)

    return lax.fori_loop(0, count - 1, turn, running)


def head_major(tensor, head_count):
    return tensor.reshape(tensor.shape[0], head_count, -1).transpose(1, 0, 2)


def householder_block(householder, head_count):
    vectors = head_major(householder.astype(jnp.float32), head_count)
    reflect_directions = vectors * lax.rsqrt(
        jnp.sum(vectors * vectors, axis=-1, keepdims=True) + 1e-06
    )
    row_total = reflect_directions.shape[1]
    head_width = reflect_directions.shape[2]
    gram_matrix = jnp.einsum(
        "jsi,jri->jsr", reflect_directions, reflect_directions, precision=precise_setting
    )
    strict = jnp.tril(jnp.ones((row_total, row_total), dtype=bool), -1)
    lower_mat = jnp.eye(row_total, dtype=jnp.float32) + 2.0 * jnp.where(strict, gram_matrix, 0.0)
    solver = jax.vmap(
        lambda tri_mat, rhs_mat: jax.scipy.linalg.solve_triangular(
            tri_mat, rhs_mat, lower=True, unit_diagonal=True
        )
    )
    update_terms = 2.0 * solver(lower_mat, reflect_directions)
    product = jnp.eye(head_width, dtype=jnp.float32) - jnp.einsum(
        "hld,hle->hde", update_terms, reflect_directions, precision=precise_setting
    )
    return (reflect_directions, update_terms, product)


def turn_forward(value_rows, reflect_directions, update_terms, prefix_mat):
    row_total = value_rows.shape[1]
    inclusive_mask = jnp.tril(jnp.ones((row_total, row_total), dtype=bool))
    reflect_coefficients = jnp.where(
        inclusive_mask,
        jnp.einsum("otu,oku->otk", value_rows, reflect_directions, precision=precise_setting),
        0.0,
    )
    within_block_part = value_rows - jnp.einsum(
        "xvw,xws->xvs", reflect_coefficients, update_terms, precision=precise_setting
    )
    return jnp.einsum("hie,hde->hid", within_block_part, prefix_mat, precision=precise_setting)


def turn_backward(grad_rows, reflect_directions, update_terms, prefix_mat):
    row_total = grad_rows.shape[1]
    inclusive_mask = jnp.tril(jnp.ones((row_total, row_total), dtype=bool))
    reflected_rows = jnp.einsum("hid,hde->hie", grad_rows, prefix_mat, precision=precise_setting)
    reflect_coefficients = jnp.where(
        inclusive_mask,
        jnp.einsum("hie,hme->him", reflected_rows, update_terms, precision=precise_setting),
        0.0,
    )
    return reflected_rows - jnp.einsum(
        "xvw,xws->xvs", reflect_coefficients, reflect_directions, precision=precise_setting
    )


def compose(earlier, latter):
    return jnp.einsum("hde,hef->hdf", earlier, latter, precision=precise_setting)


def project(grad_rows, weight):
    return lax.dot_general(
        grad_rows, weight, (((1,), (1,)), ((), ())), preferred_element_type=jnp.float32
    )


def on_device(query, key, value, householder, cotangent, w_query, w_key, w_value):
    tok_rows, width_dev = query.shape
    heads_dev = width_dev // HEAD_DIM
    cycle_place = lax.axis_index("ctx")
    reflect_directions, update_terms, product = householder_block(householder, heads_dev)
    identity_mat = jnp.broadcast_to(
        jnp.eye(HEAD_DIM, dtype=jnp.float32), (heads_dev, HEAD_DIM, HEAD_DIM)
    )
    prefix_mat = prefix(product, "ctx", compose, identity_mat)
    q_turned = turn_forward(
        head_major(query.astype(jnp.float32), heads_dev),
        reflect_directions,
        update_terms,
        prefix_mat,
    ).astype(jnp.bfloat16)
    k_turned = turn_forward(
        head_major(key.astype(jnp.float32), heads_dev), reflect_directions, update_terms, prefix_mat
    ).astype(jnp.bfloat16)
    q_rows = q_turned.transpose(1, 0, 2).reshape(tok_rows, width_dev)
    k_rows = k_turned.transpose(1, 0, 2).reshape(tok_rows, width_dev)
    keys_all, values_all = (
        lax.all_gather(k_rows, "ctx", axis=0, tiled=True),
        lax.all_gather(value, "ctx", axis=0, tiled=True),
    )
    total_rows = keys_all.shape[0]
    key_span = 4 * tok_rows
    block_count = total_rows // key_span
    first_place = cycle_place * tok_rows
    last_place = first_place + tok_rows - 1
    q_places = first_place + jnp.arange(tok_rows)
    query_split = q_rows.reshape(tok_rows, heads_dev, HEAD_DIM)
    cotan_split = cotangent.reshape(tok_rows, heads_dev, HEAD_DIM)
    scale_factor = HEAD_DIM ** (-0.5)

    def key_block(row_start):
        key_piece = lax.dynamic_slice_in_dim(keys_all, row_start, key_span, 0).reshape(
            key_span, heads_dev, HEAD_DIM
        )
        value_piece = lax.dynamic_slice_in_dim(values_all, row_start, key_span, 0).reshape(
            key_span, heads_dev, HEAD_DIM
        )
        key_places = row_start + jnp.arange(key_span)
        scores = (
            jnp.einsum("ihd,jhd->hij", query_split, key_piece, preferred_element_type=jnp.float32)
            * scale_factor
        )
        causal = key_places[None, :] <= q_places[:, None]
        return (key_piece, value_piece, scores, causal)

    def stats_step(softmax_state, block_index):
        row_start = block_index * key_span

        def stats_live_block(passed):
            running_max, running_total = passed
            _, _, scores, causal = key_block(row_start)
            scores = jnp.where(causal[None], scores, -1e30)
            new_max = jnp.maximum(running_max, jnp.max(scores, axis=2))
            new_total = running_total * jnp.exp(running_max - new_max) + jnp.sum(
                jnp.exp(scores - new_max[:, :, None]), axis=2
            )
            return (new_max, new_total)

        return (
            lax.cond(
                row_start <= last_place, stats_live_block, lambda passed: passed, softmax_state
            ),
            None,
        )

    start_state = (
        jnp.full((heads_dev, tok_rows), -1e30, jnp.float32),
        jnp.zeros((heads_dev, tok_rows), jnp.float32),
    )
    (running_max, running_total), _ = lax.scan(stats_step, start_state, jnp.arange(block_count))
    log_total = running_max + jnp.log(running_total)

    def probabilities(row_start):
        key_piece, value_piece, scores, causal = key_block(row_start)
        soft_weights = jnp.where(causal[None], jnp.exp(scores - log_total[:, :, None]), 0.0)
        return (key_piece, value_piece, soft_weights)

    def out_step(current_sum, block_index):
        row_start = block_index * key_span

        def out_live_block(passed):
            _, value_piece, soft_weights = probabilities(row_start)
            return passed + jnp.einsum(
                "hij,jhd->ihd",
                soft_weights.astype(jnp.bfloat16),
                value_piece,
                preferred_element_type=jnp.float32,
            )

        return (
            lax.cond(row_start <= last_place, out_live_block, lambda passed: passed, current_sum),
            None,
        )

    attended, _ = lax.scan(
        out_step, jnp.zeros((tok_rows, heads_dev, HEAD_DIM), jnp.float32), jnp.arange(block_count)
    )
    delta_row = jnp.sum(cotan_split.astype(jnp.float32) * attended, axis=2).T
    empty_sum = jnp.zeros((tok_rows, heads_dev, HEAD_DIM), jnp.float32)

    def joint_step(current_sum, block_index):
        row_start = block_index * key_span

        def joint_live_block(passed):
            key_piece, value_piece, soft_weights = probabilities(row_start)
            weights_low = soft_weights.astype(jnp.bfloat16)
            grad_weights = jnp.einsum(
                "ihd,jhd->hij", cotan_split, value_piece, preferred_element_type=jnp.float32
            )
            grad_scores = (soft_weights * (grad_weights - delta_row[:, :, None])).astype(
                jnp.bfloat16
            )
            new_sum = passed + jnp.einsum(
                "hij,jhd->ihd", grad_scores, key_piece, preferred_element_type=jnp.float32
            )
            grad_k = (
                jnp.einsum(
                    "hij,ihd->jhd", grad_scores, query_split, preferred_element_type=jnp.float32
                )
                * scale_factor
            )
            grad_v = jnp.einsum(
                "hij,ihd->jhd", weights_low, cotan_split, preferred_element_type=jnp.float32
            )
            rows_out = jnp.concatenate(
                [grad_k.reshape(key_span, -1), grad_v.reshape(key_span, -1)], axis=1
            )
            return (new_sum, rows_out)

        def dead_block(passed):
            return (passed, jnp.zeros((key_span, 2 * width_dev), jnp.float32))

        return lax.cond(row_start <= last_place, joint_live_block, dead_block, current_sum)

    grad_q_sum, term_blocks = lax.scan(joint_step, empty_sum, jnp.arange(block_count))
    all_terms = term_blocks.reshape(total_rows, 2 * width_dev)
    key_grads = lax.psum_scatter(all_terms, "ctx", scatter_dimension=0, tiled=True)
    grad_q_turned = grad_q_sum * scale_factor
    grad_k_turned = (
        key_grads[:, :width_dev].reshape(tok_rows, heads_dev, HEAD_DIM).transpose(1, 0, 2)
    )
    grad_value = key_grads[:, width_dev:].astype(jnp.bfloat16)
    grad_query = turn_backward(
        grad_q_turned.transpose(1, 0, 2), reflect_directions, update_terms, prefix_mat
    )
    grad_query = grad_query.transpose(1, 0, 2).reshape(tok_rows, width_dev).astype(jnp.bfloat16)
    grad_key = turn_backward(grad_k_turned, reflect_directions, update_terms, prefix_mat)
    grad_key = grad_key.transpose(1, 0, 2).reshape(tok_rows, width_dev).astype(jnp.bfloat16)
    partial_grad = (
        project(grad_query, w_query) + project(grad_key, w_key) + project(grad_value, w_value)
    )
    return lax.psum_scatter(
        partial_grad.astype(jnp.bfloat16), "head", scatter_dimension=1, tiled=True
    ).astype(jnp.float32)


def solution(mesh):
    return jax.shard_map(
        on_device,
        mesh=mesh,
        in_specs=(
            P("ctx", "head"),
            P("ctx", "head"),
            P("ctx", "head"),
            P("ctx", "head"),
            P("ctx", "head"),
            P(None, "head"),
            P(None, "head"),
            P(None, "head"),
        ),
        out_specs=P("ctx", "head"),
        check_vma=False,
    )
```

profile of v0, /device:TPU:1, one launch (start us, length us, event | category | flops | bytes accessed | tf_op | source)
XLA Modules:
  0.0 813.4 jit_solution(13741482036784725759)
XLA Ops:
  9.4 5.6 while.58
  15.1 40.8 %custom-call.4 = f32[2,2,128,128]{2,3,1,0:T(8,128)} custom-call(f32[2,2,128,128]{3,2,1,0:T(8,128)} %bitcast.193), custom_call_target="InvertDiagBlocksLowerTriangular" | custom-call | tf_op jit(solution)/shard_map/vmap(jit(_solve_triangular))/triangular_solve | solution.py:41
  62.1 81.2 %all-gather.9.cloned.1.call-done = f32[64,128,128]{2,1,0:T(8,128)} async-done(((f32[2,128,128]{2,1,0:T(8,128)}), f32[64,128,128]{2,1,0:T(8,128)}) %all-gather.9.cloned.1.call-update) | async-done | bytes 4194320 | tf_op jit(solution)/shard_map/all_gather | solution.py:14
  143.3 41.7 %while.57 = (s32[]{:T(128)}, f32[2,128,128]{1,2,0:T(8,128)S(1)}, s32[]{:T(128)}, f32[32,2,128,128]{3,2,1,0:T(8,128)}, s32[]{:T(128)}) while((s32[]{:T(128)}, f32[2,128,128]{1,2,0:T(8,128)S(1)}, s32[]{:T(128)}, f32[32,2,128,128]{3,2,1,0:T(8,128)}, s32[]{:T(128)}) %tuple.179), condition=%wide.region_2.3_spmd, body=%wide.region_1.2_spmd.sunk | while | flops 50364416 | bytes 787015 | solution.py:21
  192.7 73.6 %all-gather.5.cloned.1.call-done = bf16[8192,256]{0,1:T(8,128)(2,1)} async-done(((bf16[256,256]{0,1:T(8,128)(2,1)}), bf16[8192,256]{0,1:T(8,128)(2,1)}) %all-gather.5.cloned.1.call-update) | async-done | bytes 4194320 | tf_op jit(solution)/shard_map/all_gather | solution.py:111
  266.2 14.3 %while.59 = (s32[]{:T(128)}, f32[2,256]{1,0:T(2,128)S(1)}, f32[2,256]{1,0:T(2,128)S(1)}, s32[8]{0:T(128)S(1)}, s32[]{:T(128)}, /*index=5*/bf16[8192,256]{0,1:T(8...) while((s32[]{:T(128)}, f32[2,256]{1,0:T(2,128)S(1)}, ...), condition=%wide.region_8.9_spmd.clone, body=%wide.region_3.8_spmd.clone.sunk | while | flops 138152192 | bytes 6723865 | solution.py:163
  267.6 3.5 conditional.9
  280.6 71.6 %all-gather.7.cloned.1.call-done = bf16[8192,256]{0,1:T(8,128)(2,1)} async-done(((bf16[256,256]{0,1:T(8,128)(2,1)}), bf16[8192,256]{0,1:T(8,128)(2,1)}) %all-gather.7.cloned.1.call-update) | async-done | bytes 4194320 | tf_op jit(solution)/shard_map/all_gather | solution.py:112
  352.9 16.8 %while.60 = (s32[]{:T(128)}, f32[256,2,128]{0,2,1:T(8,128)}, s32[8]{0:T(128)S(1)}, s32[]{:T(128)}, bf16[8192,256]{0,1:T(8,128)(2,1)}, /*index=5*/bf16[8192,256]{...) while((s32[]{:T(128)}, f32[256,2,128]{0,2,1:T(8,128)}, ...), condition=%wide.region_12.13_spmd.clone, body=%wide.region_9.12_spmd.clone.sunk | while | flops 270861568 | bytes 4339977 | solution.py:188
  354.3 5.5 conditional.10
  370.7 75.9 %while.61 = (s32[]{:T(128)}, f32[256,2,128]{0,2,1:T(8,128)S(1)}, f32[8,1024,512]{2,1,0:T(8,128)}, s32[8]{0:T(128)S(1)}, s32[]{:T(128)}, /*index=5*/bf16[8192,256...) while((s32[]{:T(128)}, f32[256,2,128]{0,2,1:T(8,128)S(1)}, ...), condition=%wide.region_17.18_spmd.clone, body=%wide.region_14.17_spmd.clone.sunk | while | flops 675874048 | bytes 29901652 | solution.py:228
  372.0 6.2 conditional.11
  378.1 2.9 copy.193
  381.1 3.1 constant_dynamic-update-slice_fusion.2
  387.1 2.9 copy.193
  390.0 3.1 constant_dynamic-update-slice_fusion.2
  396.0 2.9 copy.193
  398.9 3.1 constant_dynamic-update-slice_fusion.2
  404.9 2.9 copy.193
  407.8 3.2 constant_dynamic-update-slice_fusion.2
  413.9 2.9 copy.193
  416.8 3.1 constant_dynamic-update-slice_fusion.2
  422.8 2.9 copy.193
  425.8 3.1 constant_dynamic-update-slice_fusion.2
  431.7 2.9 copy.193
  434.7 3.1 constant_dynamic-update-slice_fusion.2
  440.6 2.9 copy.193
  443.6 3.1 constant_dynamic-update-slice_fusion.2
  449.3 2.7 fusion.63
  452.0 308.6 %reduce-scatter.3.cloned.1.call-done = f32[256,512]{1,0:T(8,128)} async-done(((f32[8192,512]{1,0:T(8,128)}), f32[256,512]{1,0:T(8,128)}) %reduce-scatter.3.cloned.1.call-update) | async-done | bytes 524304 | tf_op jit(solution)/shard_map/reduce_scatter | solution.py:230
  763.6 3.1 convolution_add_fusion.1
  768.8 36.2 %reduce-scatter.5.cloned.1.call-done = bf16[256,512]{1,0:T(8,128)(2,1)} async-done(((bf16[256,4096]{1,0:T(8,128)(2,1)}), bf16[256,512]{1,0:T(8,128)(2,1)}) %reduce-scatter.5.cloned.1.call-update) | async-done | bytes 262160 | tf_op jit(solution)/shard_map/reduce_scatter | solution.py:245
  (270 shorter events, 126.9 us)
Async XLA Ops:
  6.5 442.7 %copy-start = (bf16[4096,256]{1,0:T(8,128)(2,1)S(1)}, bf16[4096,256]{1,0:T(8,128)(2,1)}, u32[]{:S(2)}) copy-start(bf16[4096,256]{1,0:T(8,128)(2,1)} %param.27) | copy-start | bytes 6291460
  6.5 136.8 %all-gather.9.cloned.1.call-start = ((), (), s32[]{:S(2)}) async-start(), calls=%async_computation.6 | async-start | bytes 4325376 | tf_op jit(solution)/shard_map/all_gather | solution.py:14
  9.4 49.4 %copy-start.12 = (f32[128,128]{1,0:T(8,128)S(1)}, f32[128,128]{1,0:T(8,128)}, u32[]{:S(2)}) copy-start(f32[128,128]{1,0:T(8,128)} %fusion.50) | copy-start | bytes 196612
  15.1 45.3 %copy-start.14 = (bf16[256,256]{1,0:T(8,128)(2,1)S(1)}, bf16[256,256]{1,0:T(8,128)(2,1)}, u32[]{:S(2)}) copy-start(bf16[256,256]{1,0:T(8,128)(2,1)} %param.23) | copy-start | bytes 393220
  57.1 131.7 %copy-start.3 = (f32[2,128,128]{2,1,0:T(8,128)}, f32[2,128,128]{2,1,0:T(8,128)S(1)}, u32[]{:S(2)}) copy-start(f32[2,128,128]{2,1,0:T(8,128)S(1)} %fusion.45) | copy-start | bytes 393220
  58.9 130.0 %copy-start.6 = (f32[2,128,128]{2,1,0:T(8,128)}, f32[2,128,128]{2,1,0:T(8,128)S(1)}, u32[]{:S(2)}) copy-start(f32[2,128,128]{2,1,0:T(8,128)S(1)} %fusion.44) | copy-start | bytes 393220
  60.2 206.0 %all-gather.5.cloned.1.call-start = ((), (), s32[]{:S(2)}) async-start(), calls=%async_computation.2 | async-start | bytes 4325376 | tf_op jit(solution)/shard_map/all_gather | solution.py:111
  60.6 127.9 %copy-start.10 = (pred[256,256]{0,1:T(8,128)(4,1)}, pred[256,256]{0,1:T(8,128)(4,1)S(1)}, u32[]{:S(2)}) copy-start(pred[256,256]{0,1:T(8,128)(4,1)S(1)} %iota_compare_fusion.3) | copy-start | bytes 196612
  143.3 42.9 %copy-start.15 = (bf16[256,256]{1,0:T(8,128)(2,1)S(1)}, bf16[256,256]{1,0:T(8,128)(2,1)}, u32[]{:S(2)}) copy-start(bf16[256,256]{1,0:T(8,128)(2,1)} %param.24) | copy-start | bytes 393220
  143.3 43.9 %copy-start.16 = (bf16[256,256]{1,0:T(8,128)(2,1)S(1)}, bf16[256,256]{1,0:T(8,128)(2,1)}, u32[]{:S(2)}) copy-start(bf16[256,256]{1,0:T(8,128)(2,1)} %param.22) | copy-start | bytes 393220
  185.0 6.0 copy-start.1
  186.1 166.0 %all-gather.7.cloned.1.call-start = ((), (), s32[]{:S(2)}) async-start(), calls=%async_computation.3 | async-start | bytes 4325376 | tf_op jit(solution)/shard_map/all_gather | solution.py:112
  187.0 573.6 %reduce-scatter.3.cloned.1.call-start = ((), (), s32[]{:S(2)}) async-start(), calls=%async_computation.4 | async-start | bytes 17301504 | tf_op jit(solution)/shard_map/reduce_scatter | solution.py:230
  372.0 2.2 copy-start.5
  446.6 0.9 copy-start.2
  446.6 1.3 copy-start.4
  446.6 1.3 copy-start.7
  446.6 1.3 copy-start.11
  446.7 358.4 %reduce-scatter.5.cloned.1.call-start = ((), (), s32[]{:S(2)}) async-start(), calls=%async_computation.5 | async-start | bytes 2359296 | tf_op jit(solution)/shard_map/reduce_scatter | solution.py:245
  761.8 1.7 copy-start.8
  763.6 3.1 copy-start.9
  763.6 3.1 copy-start.13
Sparse Core Ops, SparseCore 0:
  60.3 82.9 all-gather.8
  186.3 79.9 all-gather.4
  268.7 83.3 all-gather.6
  446.8 313.7 reduce-scatter.2
  769.0 36.0 reduce-scatter.4
where the time goes:
time: 818 us; the launch traced here: 813 us
  waiting for transfers between devices  571 us (70%)
  local copies, waits for them, and re-layouts  93.7 us (11%)
  matrix products  68 us (8%)
  other arithmetic  48 us (6%)
  loops' own time  18.2 us (2%)
  between operations  13.6 us (2%)
    reduce_scatter x1, waiting for transfers between devices, on_device(): lax.psum_scatter(all_terms, 'ctx', scatter_dimension=0, tiled=True)  309 us
    all_gather x1, waiting for transfers between devices, prefix(): pieces = lax.all_gather(value, axis)  81.2 us
    all_gather x1, waiting for transfers between devices, on_device(): lax.all_gather(k_rows, 'ctx', axis=0, tiled=True)  73.6 us
    all_gather x1, waiting for transfers between devices, on_device(): lax.all_gather(value, 'ctx', axis=0, tiled=True)  71.6 us
    dynamic_update_slice x16, local copies, waits for them, and re-layouts, on_device(): lax.scan(joint_step, empty_sum, jnp.arange(block_count))  48.4 us
    another operation x5, other arithmetic, householder_block(): jax.scipy.linalg.solve_triangular(tri_mat, rhs_mat, lower=True, unit_diag...  40.9 us
    dot_general x31, matrix products, compose(): jnp.einsum('hde,hef->hdf', earlier, latter, precision=precise_setting)  40.2 us
    reduce_scatter x1, waiting for transfers between devices, on_device(): lax.psum_scatter(partial_grad.astype(jnp.bfloat16), 'head', scatter_dimen...  36.2 us
  transfers between devices with their start and end apart: 5, of which 5 were waited for; matrix products, arithmetic and copies ran while one was open for 3% of the time, Pallas kernels for 0%

commit v1 on v0

v1 whole, which is shorter than its diff:
```python
import functools
import math

import jax
import jax.numpy as jnp
from jax import lax
from jax.experimental import pallas as pl
from jax.experimental.pallas import tpu as pltpu
from jax.sharding import PartitionSpec as P

MESH = pl.DeviceIdType.MESH
BF = jnp.bfloat16
F32 = jnp.float32
ROWS = 256
HD = 128
NZ, NX = 8, 4
SCALE = HD**-0.5
SCALE2 = SCALE * math.log2(math.e)
VMEM_BYTES = 56 * 1024 * 1024
LOW = -1e30


def nn(a, b):
    return lax.dot_general(a, b, (((1,), (0,)), ((), ())), preferred_element_type=F32)


def nt(a, b):
    return lax.dot_general(a, b, (((1,), (1,)), ((), ())), preferred_element_type=F32)


def split(a):
    high = a.astype(BF)
    return high, (a - high.astype(F32)).astype(BF)


def nn3(a, b):
    ah, al = split(a)
    bh, bl = split(b)
    return nn(ah, bh) + (nn(al, bh) + nn(ah, bl))


def nt3(a, b):
    ah, al = split(a)
    bh, bl = split(b)
    return nt(ah, bh) + (nt(al, bh) + nt(ah, bl))


def iotas(shape):
    return lax.broadcasted_iota(jnp.int32, shape, 0), lax.broadcasted_iota(jnp.int32, shape, 1)


def identity():
    row, col = iotas((HD, HD))
    return jnp.where(row == col, 1.0, 0.0).astype(F32)


def place():
    me = lax.axis_index("ctx")
    return me // NX, me % NX


def meet(peers, axis):
    barrier = pltpu.get_barrier_semaphore()
    for peer in peers:
        pl.semaphore_signal(barrier, inc=1, device_id={axis: peer}, device_id_type=MESH)
    pl.semaphore_wait(barrier, len(peers))


def send(src, dst, send_sem, recv_sem, peer, axis="ctx"):
    return pltpu.make_async_remote_copy(
        src_ref=src,
        dst_ref=dst,
        send_sem=send_sem,
        recv_sem=recv_sem,
        device_id={axis: peer},
        device_id_type=MESH,
    )


def reflectors(hh, units, updates, products, lowers, inverses):
    row, col = iotas((HD, HD))
    chunks = [(a, b, slice(b * HD, (b + 1) * HD)) for a in range(2) for b in range(2)]
    for i, (a, b, rows) in enumerate(chunks):
        vec = hh[rows, a * HD : (a + 1) * HD].astype(F32)
        unit = vec * lax.rsqrt(jnp.sum(vec * vec, axis=1, keepdims=True) + 1e-6)
        lower = 2.0 * jnp.where(row > col, nt3(unit, unit), 0.0)
        units[a, rows] = unit
        lowers[i] = lower
        inverses[i] = identity() - jnp.where(row // 2 == col // 2, lower, 0.0)

    def join(level, carry):
        row_part, col_part = lax.shift_right_logical(row, level), lax.shift_right_logical(col, level)
        pick = (row_part == col_part + 1) & ((col_part & 1) == 0)
        for i in range(4):
            inverse = inverses[i]
            inner = nn3(jnp.where(pick, lowers[i], 0.0), inverse)
            inverses[i] = inverse - nn3(inverse, inner)
        return carry

    lax.fori_loop(1, 7, join, 0)
    for i, (a, b, rows) in enumerate(chunks):
        unit, inverse = units[a, rows], inverses[i]
        updates[a, rows] = 2.0 * nn3(inverse, unit)
        turned = 2.0 * nt3(unit.T, inverse)
        products[a, b] = identity() - nn3(turned, unit)


def gather_kernel(
    hh, q, k, v, c,
    qg, cg, kg, vg, units, updates, prefixes,
    qs, ks, cs, vs, px, tz, qlocal, klocal, products, lowers, inverses, totals,
    zs, zr, xs, xr, ps, pr, ts, tr, os, orr,
):
    z, x = place()
    head = z // 4
    line = [(z + d) % NZ for d in range(1, NZ)]
    cross = [(x + d) % NX for d in range(1, NX)]
    other = NZ - 1 - z
    x_rows = pl.ds(pl.multiple_of(x * ROWS, ROWS), ROWS)
    meet([zz * NX + x for zz in line] + [z * NX + xx for xx in cross], "ctx")

    def line_copies(src, dst, i):
        return [
            send(src.at[zz // 4], dst.at[z], zs.at[i, d], zr.at[i, d], zz * NX + x)
            for d, zz in enumerate(line)
        ]

    def pair_copy(src, dst, i):
        return send(
            src.at[1 - head], dst.at[head, x_rows], os.at[i], orr.at[i], other * NX + x
        )

    def cross_copies(dst, slot, i):
        return [
            send(dst.at[slot, x_rows], dst.at[slot, x_rows], xs.at[i, d], xr.at[i, d], z * NX + xx)
            for d, xx in enumerate(cross)
        ]

    for part in range(2):
        cols = slice(part * HD, (part + 1) * HD)
        cs[part] = c[:, cols]
        vs[part] = v[:, cols]
    c_copies = line_copies(cs, cg, 0)
    v_pair = pair_copy(vs, vg, 0)
    v_pair.start()
    for copy in c_copies:
        copy.start()
    cg[z] = cs[head]
    vg[head, x_rows] = vs[head]
    v_cross = cross_copies(vg, head, 0)
    for copy in v_cross:
        copy.start()

    reflectors(hh, units, updates, products, lowers, inverses)
    for a in range(2):
        px[x, a] = nn3(products[a, 0], products[a, 1])
    p_cross = [
        send(px.at[x], px.at[x], ps.at[d], pr.at[d], z * NX + xx) for d, xx in enumerate(cross)
    ]
    for copy in p_cross:
        copy.start()

    v_pair.wait()
    v_cross2 = cross_copies(vg, 1 - head, 1)
    for copy in v_cross2:
        copy.start()

    row, col = iotas((HD, HD))
    for a in range(2):
        for b in range(2):
            rows = slice(b * HD, (b + 1) * HD)
            for src, dst in ((q, qlocal), (k, klocal)):
                part = src[rows, a * HD : (a + 1) * HD].astype(F32)
                coef = jnp.where(row >= col, nt3(part, units[a, rows]), 0.0)
                dst[a, rows] = part - nn3(coef, updates[a, rows])

    for copy in p_cross:
        copy.wait()
    for a in range(2):
        one = px[0, a]
        two = nn3(one, px[1, a])
        three = nn3(two, px[2, a])
        tz[z, a] = nn3(three, px[3, a])
        prefixes[a, 0] = jnp.where(
            x == 0, identity(), jnp.where(x == 1, one, jnp.where(x == 2, two, three))
        )
    t_line = [
        send(tz.at[z], tz.at[z], ts.at[d], tr.at[d], zz * NX + x) for d, zz in enumerate(line)
    ]
    for d in range(1, NZ):

        @pl.when(z + d < NZ)
        def _(d=d):
            t_line[d - 1].start()

    for d in range(1, NZ):

        @pl.when(z - d >= 0)
        def _(d=d):
            t_line[d - 1].wait_recv()

    for a in range(2):
        totals[a] = identity()

    def chain(j, carry):
        for a in range(2):
            totals[a] = nn3(totals[a], tz[j, a])
        return carry

    lax.fori_loop(0, z, chain, 0)
    for a in range(2):
        first = nn3(totals[a], prefixes[a, 0])
        second = nn3(first, products[a, 0])
        prefixes[a, 0] = first
        prefixes[a, 1] = second
        for b, prefix in enumerate((first, second)):
            rows = slice(b * HD, (b + 1) * HD)
            ks[a, rows] = nt3(klocal[a, rows], prefix).astype(BF)
            qs[a, rows] = nt3(qlocal[a, rows], prefix).astype(BF)

    k_pair = pair_copy(ks, kg, 1)
    k_pair.start()
    kg[head, x_rows] = ks[head]
    k_cross = cross_copies(kg, head, 2)
    for copy in k_cross:
        copy.start()
    q_copies = line_copies(qs, qg, 1)
    for copy in q_copies:
        copy.start()
    qg[z] = qs[head]
    k_pair.wait()
    k_cross2 = cross_copies(kg, 1 - head, 3)
    for copy in k_cross2:
        copy.start()
    for d in range(1, NZ):

        @pl.when(z + d < NZ)
        def _(d=d):
            t_line[d - 1].wait_send()

    for copy in c_copies + v_cross + v_cross2 + k_cross + q_copies + k_cross2:
        copy.wait()


def full_tile(n, low_row):
    in_low = n < NZ - 1 - low_row
    return jnp.where(in_low, low_row + 1 + n, n + 1), jnp.where(in_low, 0, 1)


def forward_kernel(qg, cg, kg, vg, top, total, delta, s_scr):
    z, x = place()
    low_row = jnp.minimum(z, NZ - 1 - z)
    top[...] = jnp.full(top.shape, LOW, F32)
    total[...] = jnp.zeros(total.shape, F32)
    delta[...] = jnp.zeros(delta.shape, F32)

    def join(row, peak, weight, moment):
        at = pl.ds(row, 1)
        old = top[at, :]
        new = jnp.maximum(old, peak)
        keep, take = jnp.exp2(old - new), jnp.exp2(peak - new)
        top[at, :] = new
        total[at, :] = total[at, :] * keep + weight * take
        delta[at, :] = delta[at, :] * keep + moment * take

    def full(n, carry):
        row, slot = full_tile(n, low_row)
        query, cot = qg[row], cg[row]
        peak = None
        for j in range(NX):
            rows = slice(j * ROWS, (j + 1) * ROWS)
            score = nt(kg[slot, rows], query) * SCALE2
            s_scr[rows] = score
            mine = jnp.max(score, axis=0, keepdims=True)
            peak = mine if peak is None else jnp.maximum(peak, mine)
        weight = moment = jnp.zeros((1, ROWS), F32)
        for j in range(NX):
            rows = slice(j * ROWS, (j + 1) * ROWS)
            p = jnp.exp2(s_scr[rows] - peak)
            weight = weight + jnp.sum(p, axis=0, keepdims=True)
            moment = moment + jnp.sum(p * nt(vg[slot, rows], cot), axis=0, keepdims=True)
        join(row, peak, weight, moment)
        return carry

    lax.fori_loop(0, NZ - 1, full, 0)

    def edge(n, carry):
        slot, j = n % 2, n // 2
        row = jnp.where(slot == 0, low_row, NZ - 1 - low_row)
        rows = pl.ds(pl.multiple_of(j * ROWS, ROWS), ROWS)
        key_at, query_at = iotas((ROWS, ROWS))
        live = key_at + j * ROWS <= query_at + x * ROWS
        score = jnp.where(live, nt(kg[slot, rows], qg[row]) * SCALE2, LOW)
        peak = jnp.max(score, axis=0, keepdims=True)
        p = jnp.where(live, jnp.exp2(score - peak), 0.0)
        moment = jnp.sum(p * nt(vg[slot, rows], cg[row]), axis=0, keepdims=True)
        join(row, peak, jnp.sum(p, axis=0, keepdims=True), moment)
        return carry

    lax.fori_loop(0, 2 * (x + 1), edge, 0)


def stats_kernel(top, total, delta, log_total, delta_row, held, ss, sr):
    z, x = place()
    half = z // 4
    peers = [(half * 4 + (z + d) % 4) * NX + x for d in range(1, 4)]
    meet(peers, "ctx")
    held[z % 4, 0] = top[...]
    held[z % 4, 1] = total[...]
    held[z % 4, 2] = delta[...]
    copies = [
        send(held.at[z % 4], held.at[z % 4], ss.at[d], sr.at[d], peer)
        for d, peer in enumerate(peers)
    ]
    for copy in copies:
        copy.start()
    for copy in copies:
        copy.wait()
    peak = held[0, 0]
    for i in range(1, 4):
        peak = jnp.maximum(peak, held[i, 0])
    weight = moment = jnp.zeros(peak.shape, F32)
    for i in range(4):
        take = jnp.exp2(held[i, 0] - peak)
        weight = weight + held[i, 1] * take
        moment = moment + held[i, 2] * take
    log_total[...] = peak + jnp.log2(weight)
    delta_row[...] = moment / weight


def backward_kernel(qg, cg, kg, vg, log_total, delta_row, dqt, dkv, kt, dq_acc, dk_acc, dv_acc):
    z, x = place()
    low_row = jnp.minimum(z, NZ - 1 - z)
    dq_acc[...] = jnp.zeros(dq_acc.shape, F32)
    dk_acc[...] = jnp.zeros(dk_acc.shape, F32)
    dv_acc[...] = jnp.zeros(dv_acc.shape, F32)
    for slot in range(2):
        for j in range(NX):
            rows = slice(j * ROWS, (j + 1) * ROWS)
            kt[slot, j] = kg[slot, rows].T

    def tile(row, slot, j, rows, live):
        key, query, cot = kg[slot, rows], qg[row], cg[row]
        at = pl.ds(row, 1)
        score = nt(key, query) * SCALE2 - log_total[at, :]
        if live is not None:
            score = jnp.where(live, score, LOW)
        p = jnp.exp2(score)
        grad = (p * (nt(vg[slot, rows], cot) - delta_row[at, :])).astype(BF)
        dv_acc[slot, rows] += nn(p.astype(BF), cot)
        dk_acc[slot, rows] += nn(grad, query)
        return nn(kt[slot, j], grad)

    def full(n, carry):
        row, slot = full_tile(n, low_row)
        total = None
        for j in range(NX):
            part = tile(row, slot, j, slice(j * ROWS, (j + 1) * ROWS), None)
            total = part if total is None else total + part
        dq_acc[row] += total
        return carry

    lax.fori_loop(0, NZ - 1, full, 0)

    def edge(n, carry):
        slot, j = n % 2, n // 2
        row = jnp.where(slot == 0, low_row, NZ - 1 - low_row)
        rows = pl.ds(pl.multiple_of(j * ROWS, ROWS), ROWS)
        key_at, query_at = iotas((ROWS, ROWS))
        live = key_at + j * ROWS <= query_at + x * ROWS
        dq_acc[row] += tile(row, slot, j, rows, live)
        return carry

    lax.fori_loop(0, 2 * (x + 1), edge, 0)
    dqt[...] = (dq_acc[...] * SCALE).astype(BF)
    dkv[:, :, :HD] = (dk_acc[...] * SCALE).astype(BF)
    dkv[:, :, HD:] = dv_acc[...].astype(BF)


def reduce_kernel(dqt, dkv, rq, own, given, rx, out, zs, zr, xs, xr, os, orr):
    z, x = place()
    head = z // 4
    line = [(z + d) % NZ for d in range(1, NZ)]
    cross = [(x + d) % NX for d in range(1, NX)]
    meet([zz * NX + x for zz in line] + [z * NX + xx for xx in cross], "ctx")

    def rows_of(xx):
        return pl.ds(pl.multiple_of(xx * ROWS, ROWS), ROWS)

    x_copies = [
        [
            send(
                dkv.at[slot, rows_of(xx)], rx.at[x, i], xs.at[i, d], xr.at[i, d], z * NX + xx
            )
            for d, xx in enumerate(cross)
        ]
        for i, slot in enumerate((1 - head, head))
    ]
    for copies in x_copies:
        for copy in copies:
            copy.start()
    z_copies = [
        send(dqt.at[zz], rq.at[z], zs.at[d], zr.at[d], zz * NX + x) for d, zz in enumerate(line)
    ]
    for copy in z_copies:
        copy.start()
    rq[z] = dqt[z]
    rx[x, 0] = dkv[1 - head, rows_of(x)]
    rx[x, 1] = dkv[head, rows_of(x)]

    def summed(i):
        return (rx[0, i].astype(F32) + rx[1, i].astype(F32)) + (
            rx[2, i].astype(F32) + rx[3, i].astype(F32)
        )

    for copy in x_copies[0]:
        copy.wait()
    out[...] = summed(0).astype(BF)
    pair = send(out, given, os.at[0], orr.at[0], (NZ - 1 - z) * NX + x)
    pair.start()
    for copy in x_copies[1]:
        copy.wait()
    own[...] = summed(1)
    pair.wait()
    for copy in z_copies:
        copy.wait()


def project_kernel(
    rq, own, given, units, updates, prefixes, wq, wk, wv,
    out,
    w, grads, kv, mine, theirs, relay, landed,
    ws, cs, cr, ys, yr,
):
    z, _ = place()
    head = z // 4
    me = lax.axis_index("head")
    y, core = me // 2, me % 2
    mate = y * 2 + 1 - core
    order = [(y + d) % 4 for d in (2, 1, 3)]
    meet([mate] + [yy * 2 + core for yy in order], "head")
    loads = [pltpu.make_async_copy(src, w.at[i], ws.at[i]) for i, src in enumerate((wq, wk, wv))]
    for load in loads:
        load.start()
    kv[head] = own[...]
    kv[1 - head] = given[...].astype(F32)
    row, col = iotas((HD, HD))
    for a in range(2):
        cols = slice(a * HD, (a + 1) * HD)
        total = rq[4 * a].astype(F32)
        for i in range(1, 4):
            total = total + rq[4 * a + i].astype(F32)
        total = total.T
        grads[2, :, cols] = kv[a, :, HD:].astype(BF)
        for b in range(2):
            rows = slice(b * HD, (b + 1) * HD)
            for i, part in enumerate((total[rows], kv[a, rows, :HD])):
                back = nn3(part, prefixes[a, b])
                coef = jnp.where(row >= col, nt3(back, updates[a, rows]), 0.0)
                grads[i, rows, cols] = (back - nn3(coef, units[a, rows])).astype(BF)
    for load in loads:
        load.wait()

    def columns(block):
        at = pl.ds(pl.multiple_of(block * 512, 512), 512)
        return (
            nt(grads[0], w[0, at, :]) + nt(grads[1], w[1, at, :]) + nt(grads[2], w[2, at, :])
        )

    blocks = order + [y]
    swaps = []
    for i, yy in enumerate(blocks):
        mine[i] = columns(yy * 2 + 1 - core).astype(BF)
        swap = send(mine.at[i], theirs.at[i], cs.at[i], cr.at[i], mate, "head")
        swap.start()
        swaps.append(swap)
    hops = []
    for i, yy in enumerate(blocks):
        part = columns(yy * 2 + core)
        swaps[i].wait()
        part = part + theirs[i].astype(F32)
        if i < 3:
            relay[i] = part.astype(BF)
            hop = send(relay.at[i], landed.at[i], ys.at[i], yr.at[i], yy * 2 + core, "head")
            hop.start()
            hops.append(hop)
    for hop in hops:
        hop.wait()
        part = part
    for i in range(3):
        part = part + landed[i].astype(F32)
    out[...] = part


def call(kernel, outs, scratch, collective, in_specs, **extra):
    vmem = pl.BlockSpec(memory_space=pltpu.VMEM)
    params = dict(vmem_limit_bytes=VMEM_BYTES)
    if collective is not None:
        params.update(collective_id=collective, has_side_effects=True)
    return pl.pallas_call(
        kernel,
        out_shape=[jax.ShapeDtypeStruct(s, t) for s, t in outs],
        in_specs=[vmem if s is None else pl.BlockSpec(memory_space=s) for s in in_specs],
        out_specs=[vmem] * len(outs),
        scratch_shapes=scratch,
        compiler_params=pltpu.CompilerParams(**params),
        **extra,
    )


def on_device(query, key, value, householder, cotangent, w_query, w_key, w_value):
    dma = pltpu.SemaphoreType.DMA
    lines = ((NZ, ROWS, HD), BF)
    keys = ((2, NX * ROWS, HD), BF)
    own = pltpu.VMEM((2, ROWS, HD), BF)
    own32 = pltpu.VMEM((2, ROWS, HD), F32)
    qg, cg, kg, vg, units, updates, prefixes = call(
        gather_kernel,
        [
            lines, lines, keys, keys,
            ((2, ROWS, HD), F32), ((2, ROWS, HD), F32), ((2, 2, HD, HD), F32),
        ],
        [
            own, own, own, own,
            pltpu.VMEM((NX, 2, HD, HD), F32), pltpu.VMEM((NZ, 2, HD, HD), F32), own32, own32,
            pltpu.VMEM((2, 2, HD, HD), F32), pltpu.VMEM((4, HD, HD), F32),
            pltpu.VMEM((4, HD, HD), F32), pltpu.VMEM((2, HD, HD), F32),
            dma((2, 7)), dma((2, 7)), dma((4, 3)), dma((4, 3)), dma((3,)), dma((3,)),
            dma((7,)), dma((7,)), dma((2,)), dma((2,)),
        ],
        0,
        [None] * 5,
    )(householder, query, key, value, cotangent)
    stat = ((NZ, ROWS), F32)
    top, total, delta = call(
        forward_kernel, [stat] * 3, [pltpu.VMEM((NX * ROWS, ROWS), F32)], None, [None] * 4
    )(qg, cg, kg, vg)
    log_total, delta_row = call(
        stats_kernel,
        [stat] * 2,
        [pltpu.VMEM((4, 3, NZ, ROWS), F32), dma((3,)), dma((3,))],
        1,
        [None] * 3,
    )(top, total, delta)
    acc = pltpu.VMEM((2, NX * ROWS, HD), F32)
    dqt, dkv = call(
        backward_kernel,
        [((NZ, HD, ROWS), BF), ((2, NX * ROWS, 2 * HD), BF)],
        [pltpu.VMEM((2, NX, HD, ROWS), BF), pltpu.VMEM((NZ, HD, ROWS), F32), acc, acc],
        None,
        [None] * 6,
    )(qg, cg, kg, vg, log_total, delta_row)
    block = (ROWS, 2 * HD)
    rq, mine, given = call(
        reduce_kernel,
        [((NZ, HD, ROWS), BF), (block, F32), (block, BF)],
        [
            pltpu.VMEM((NX, 2) + block, BF), pltpu.VMEM(block, BF),
            dma((7,)), dma((7,)), dma((2, 3)), dma((2, 3)), dma((1,)), dma((1,)),
        ],
        2,
        [None] * 2,
    )(dqt, dkv)
    (result,) = call(
        project_kernel,
        [((ROWS, 512), F32)],
        [
            pltpu.VMEM((3, 4096, ROWS), BF), pltpu.VMEM((3, ROWS, ROWS), BF),
            pltpu.VMEM((2,) + block, F32),
            pltpu.VMEM((4, ROWS, 512), BF), pltpu.VMEM((4, ROWS, 512), BF),
            pltpu.VMEM((3, ROWS, 512), BF), pltpu.VMEM((3, ROWS, 512), BF),
            dma((3,)), dma((4,)), dma((4,)), dma((3,)), dma((3,)),
        ],
        3,
        [None] * 6 + [pl.ANY] * 3,
    )(rq, mine, given, units, updates, prefixes, w_query, w_key, w_value)
    return result


def solution(mesh):
    return jax.shard_map(
        on_device,
        mesh=mesh,
        in_specs=(P("ctx", "head"),) * 5 + (P(None, "head"),) * 3,
        out_specs=P("ctx", "head"),
        check_vma=False,
    )
```

time: 818 us -> 155 us (0.19)
  waiting for transfers between devices: 571 us -> 0 us
  Pallas kernels: 0 us -> 152 us
  local copies, waits for them, and re-layouts: 93.7 us -> 1.87 us
  matrix products: 68 us -> 0 us
  other arithmetic: 48 us -> 0 us
  loops' own time: 18.2 us -> 0 us
  between operations: 13.6 us -> 0.03 us
    reduce_scatter x2 -> x0, waiting for transfers between devices: 345 us -> none  [the longest x1 309 us: on_device(): lax.psum_scatter(all_terms, 'ctx', scatter_dimension=0, tiled=True)]
    all_gather x3 -> x0, waiting for transfers between devices: 226 us -> none  [the longest x1 81.2 us: prefix(): pieces = lax.all_gather(value, axis)]
    pallas_call x0 -> x6, Pallas kernels: none -> 152 us  [the longest x1 72.8 us: on_device(): call(gather_kernel, [lines, lines, keys, keys, ((2, ROWS, HD), F32), ((2,...]
    dot_general x55 -> x0, matrix products: 65 us -> none  [the longest x31 40.2 us: compose(): jnp.einsum('hde,hef->hdf', earlier, latter, precision=precise_setting)]
    dynamic_update_slice x16 -> x0, local copies, waits for them, and re-layouts: 48.4 us -> none  [on_device(): lax.scan(joint_step, empty_sum, jnp.arange(block_count))]
    another operation x5 -> x0, other arithmetic: 40.9 us -> none  [householder_block(): jax.scipy.linalg.solve_triangular(tri_mat, rhs_mat, lower=True, unit_diag...]
    dynamic_slice x27 -> x0, local copies, waits for them, and re-layouts: 20.3 us -> none  [the longest x24 15.2 us: on_device(): lax.scan(stats_step, start_state, jnp.arange(block_count))]
    another operation x29 -> x0, loops' own time: 18.2 us -> none  [the longest x1 5.85 us: on_device(): lax.scan(out_step, jnp.zeros((tok_rows, heads_dev, HEAD_DIM), jnp.float32...]
  transfers between devices with their start and end apart: 5 -> 0, of which waited for: 5 -> 0; matrix products, arithmetic and copies ran while one was open for 3% -> 0% of each run, Pallas kernels for 0% -> 0%
where the time goes in v1:
time: 155 us; the launch traced here: 154 us
  Pallas kernels  152 us (98%)
  local copies, waits for them, and re-layouts  1.87 us (1%)
    pallas_call x1, Pallas kernels, on_device(): call(gather_kernel, [lines, lines, keys, keys, ((2, ROWS, HD), F32), ((2,...  72.8 us
    pallas_call x1, Pallas kernels, on_device(): call(project_kernel, [((ROWS, 512), F32)], [pltpu.VMEM((3, 4096, ROWS), B...  26.4 us
    pallas_call x1, Pallas kernels, on_device(): call(reduce_kernel, [((NZ, HD, ROWS), BF), (block, F32), (block, BF)], [p...  26 us
    pallas_call x1, Pallas kernels, on_device(): call(backward_kernel, [((NZ, HD, ROWS), BF), ((2, NX * ROWS, 2 * HD), BF)...  11.6 us
    pallas_call x1, Pallas kernels, on_device(): call(stats_kernel, [stat] * 2, [pltpu.VMEM((4, 3, NZ, ROWS), F32), dma((3...  8.82 us
    pallas_call x1, Pallas kernels, on_device(): call(forward_kernel, [stat] * 3, [pltpu.VMEM((NX * ROWS, ROWS), F32)], No...  6.53 us

profile of v1, /device:TPU:1, one launch (start us, length us, event | category | flops | bytes accessed | tf_op | source)
XLA Modules:
  0.0 154.0 jit_solution(1809695996104906777)
XLA Ops:
  0.0 72.8 %shard_map.82 = (bf16[8,256,128]{2,1,0:T(8,128)(2,1)}, bf16[8,256,128]{2,1,0:T(8,128)(2,1)}, bf16[2,1024,128]{2,1,0:T(8,128)(2,1)}, bf16[2,1024,128]{2,1,0:T(8,1...) custom-call(bf16[256,256]{1,0:T(8,128)(2,1)} %hh.1, bf16[256,256]{1,0:T(8,128)(2,1)} %q.1, ...), custom_call_target="tpu_custom_call" | custom-call | tf_op jit(solution)/shard_map/pallas_call | solution.py:517
  72.8 6.5 %shard_map.83 = (f32[8,256]{1,0:T(8,128)}, f32[8,256]{1,0:T(8,128)}, f32[8,256]{1,0:T(8,128)}) custom-call(bf16[8,256,128]{2,1,0:T(8,128)(2,1)} %get-tuple-element.22.qg, bf16[8,256,128]{2,1,0:T(8,128)(2,1)} %get-tuple-element.23.cg, bf16[2,1024,128]{2,1,0:T(8,128)(2,1)} %get-tuple-element.24.kg, bf16[2,1024,128]{2,1,0:T(8,128)(2,1)} %get-tuple-element.25.vg), custom_call_target="tpu_custom_call" | custom-call | tf_op jit(solution)/shard_map/pallas_call | solution.py:535
  79.4 8.8 %shard_map.84 = (f32[8,256]{1,0:T(8,128)}, f32[8,256]{1,0:T(8,128)}) custom-call(f32[8,256]{1,0:T(8,128)} %get-tuple-element.26.top, f32[8,256]{1,0:T(8,128)} %get-tuple-element.27.total, f32[8,256]{1,0:T(8,128)} %get-tuple-element.28.delta), custom_call_target="tpu_custom_call" | custom-call | tf_op jit(solution)/shard_map/pallas_call | solution.py:538
  88.2 11.6 %shard_map.85 = (bf16[8,128,256]{2,1,0:T(8,128)(2,1)}, bf16[2,1024,256]{2,1,0:T(8,128)(2,1)}) custom-call(bf16[8,256,128]{2,1,0:T(8,128)(2,1)} %get-tuple-element.22.qg, bf16[8,256,128]{2,1,0:T(8,128)(2,1)} %get-tuple-element.23.cg, bf16[2,1024,128]{2,1,0:T(8,128)(2,1)} %get-tuple-element.24.kg, bf16[2,1024,128]{2,1,0:T(8,128)(2,1)} %get-tuple-element.25.vg, ...), custom_call_target="tpu_custom_call" | custom-call | tf_op jit(solution)/shard_map/pallas_call | solution.py:546
  99.8 26.0 %shard_map.86 = (bf16[8,128,256]{2,1,0:T(8,128)(2,1)}, f32[256,256]{1,0:T(8,128)}, bf16[256,256]{1,0:T(8,128)(2,1)}) custom-call(bf16[8,128,256]{2,1,0:T(8,128)(2,1)} %get-tuple-element.31.dqt, bf16[2,1024,256]{2,1,0:T(8,128)(2,1)} %get-tuple-element.32.dkv), custom_call_target="tpu_custom_call" | custom-call | tf_op jit(solution)/shard_map/pallas_call | solution.py:554
  125.8 26.4 %shard_map.87 = f32[256,512]{1,0:T(8,128)} custom-call(bf16[8,128,256]{2,1,0:T(8,128)(2,1)} %get-tuple-element.33.rq, f32[256,256]{1,0:T(8,128)} %get-tuple-element.34.own, bf16[256,256]{1,0:T(8,128)(2,1)} %get-tuple-element.35.given, f32[2,256,128]{2,1,0:T(8,128)} %get-tuple-element.36.units, f32[2,256,128]{2,1,0:T(8,128)} %get-tuple-element.37.updates, ...), custom_call_target="tpu_custom_call" | custom-call | tf_op jit(solution)/shard_map/pallas_call | solution.py:564
  152.2 1.9 %copy.10 = f32[256,512]{1,0:T(8,128)} copy(f32[256,512]{1,0:T(8,128)} %shard_map.87) | data formatting | bytes 1048576

commit v2 on v1

v2 whole, which is shorter than its diff:
```python
import math

import jax
import jax.numpy as jnp
from jax import lax
from jax.experimental import pallas as pl
from jax.experimental.pallas import tpu as pltpu
from jax.sharding import PartitionSpec as P

MESH = pl.DeviceIdType.MESH
BF = jnp.bfloat16
F32 = jnp.float32
ROWS = 256
HD = 128
NZ, NX = 8, 4
SCALE = HD**-0.5
SCALE2 = SCALE * math.log2(math.e)
VMEM_BYTES = 56 * 1024 * 1024
LOW = -1e30


def nn(a, b):
    return lax.dot_general(a, b, (((1,), (0,)), ((), ())), preferred_element_type=F32)


def nt(a, b):
    return lax.dot_general(a, b, (((1,), (1,)), ((), ())), preferred_element_type=F32)


def split(a):
    high = a.astype(BF)
    return high, (a - high.astype(F32)).astype(BF)


def nn3(a, b):
    ah, al = split(a)
    bh, bl = split(b)
    return nn(ah, bh) + (nn(al, bh) + nn(ah, bl))


def nt3(a, b):
    ah, al = split(a)
    bh, bl = split(b)
    return nt(ah, bh) + (nt(al, bh) + nt(ah, bl))


def iotas(shape):
    return lax.broadcasted_iota(jnp.int32, shape, 0), lax.broadcasted_iota(jnp.int32, shape, 1)


def identity():
    row, col = iotas((HD, HD))
    return jnp.where(row == col, 1.0, 0.0).astype(F32)


def place():
    me = lax.axis_index("ctx")
    return me // NX, me % NX


def send(src, dst, send_sem, recv_sem, peer, axis="ctx"):
    return pltpu.make_async_remote_copy(
        src_ref=src,
        dst_ref=dst,
        send_sem=send_sem,
        recv_sem=recv_sem,
        device_id={axis: peer},
        device_id_type=MESH,
    )


def reflectors(hh, units, updates, products, lowers, inverses):
    row, col = iotas((HD, HD))
    chunks = [(a, b, slice(b * HD, (b + 1) * HD)) for a in range(2) for b in range(2)]
    for i, (a, b, rows) in enumerate(chunks):
        vec = hh[rows, a * HD : (a + 1) * HD].astype(F32)
        unit = vec * lax.rsqrt(jnp.sum(vec * vec, axis=1, keepdims=True) + 1e-6)
        lower = 2.0 * jnp.where(row > col, nt3(unit, unit), 0.0)
        units[a, rows] = unit
        lowers[i] = lower
        inverses[i] = identity() - jnp.where(row // 2 == col // 2, lower, 0.0)

    def join(level, carry):
        row_part, col_part = lax.shift_right_logical(row, level), lax.shift_right_logical(col, level)
        pick = (row_part == col_part + 1) & ((col_part & 1) == 0)
        for i in range(4):
            inverse = inverses[i]
            inner = nn3(jnp.where(pick, lowers[i], 0.0), inverse)
            inverses[i] = inverse - nn3(inverse, inner)
        return carry

    lax.fori_loop(1, 7, join, 0)
    for i, (a, b, rows) in enumerate(chunks):
        unit, inverse = units[a, rows], inverses[i]
        updates[a, rows] = 2.0 * nn3(inverse, unit)
        turned = 2.0 * nt3(unit.T, inverse)
        products[a, b] = identity() - nn3(turned, unit)


def rows_at(block):
    return pl.ds(pl.multiple_of(block * ROWS, ROWS), ROWS)


def whole_kernel(
    hh, q, k, v, c, wq, wk, wv,
    out,
    qg, cg, kg, vg, units, updates, prefixes,
    qs, ks, cs, vs, px, tz, qlocal, klocal, products, lowers, inverses, totals,
    s_scr, held, log_total, delta_row,
    kt, dq_acc, dk_acc, dv_acc, dqt, dkv, rq, rx, pair_out, kv,
    w, grads, mine, theirs, relay, landed,
    zs, zr, xs, xr, ps, pr, ts, tr, fs, fr, os, orr, ss, sr, ws, ms, mr, ys, yr,
):
    z, x = place()
    me = lax.axis_index("head")
    y, core = me // 2, me % 2
    mate = y * 2 + 1 - core
    head = z // 4
    low_row = jnp.minimum(z, NZ - 1 - z)
    other = NZ - 1 - z
    line = [(z + d) % NZ for d in range(1, NZ)]
    cross = [(x + d) % NX for d in range(1, NX)]
    order = [(y + d) % 4 for d in (2, 1, 3)]
    loads = [pltpu.make_async_copy(src, w.at[i], ws.at[i]) for i, src in enumerate((wq, wk, wv))]
    for load in loads:
        load.start()
    barrier = pltpu.get_barrier_semaphore()
    peers = [{"ctx": zz * NX + x} for zz in line] + [{"ctx": z * NX + xx} for xx in cross]
    peers = peers + [{"head": mate}] + [{"head": yy * 2 + core} for yy in order]
    for peer in peers:
        pl.semaphore_signal(barrier, inc=1, device_id=peer, device_id_type=MESH)
    pl.semaphore_wait(barrier, len(peers))

    def line_copy(src, dst, i, to, source):
        return send(src.at[to // 4], dst.at[source], zs.at[i, to], zr.at[i, source], to * NX + x)

    def line_start(src, dst, i):
        def step(d, carry):
            to = (z + d) % NZ

            @pl.when(z >= jnp.minimum(to, NZ - 1 - to))
            def _():
                line_copy(src, dst, i, to, z).start()

            return carry

        lax.fori_loop(1, NZ, step, 0)

    def line_wait_send(src, dst, i):
        def step(d, carry):
            to = (z + d) % NZ

            @pl.when(z >= jnp.minimum(to, NZ - 1 - to))
            def _():
                line_copy(src, dst, i, to, z).wait_send()

            return carry

        lax.fori_loop(1, NZ, step, 0)

    def pair_copy(src, dst, i):
        return send(
            src.at[1 - head], dst.at[head, rows_at(x)], os.at[i], orr.at[i], other * NX + x
        )

    def cross_copies(dst, slot, i):
        return [
            send(dst.at[slot, rows_at(x)], dst.at[slot, rows_at(x)], xs.at[i, d], xr.at[i, d], z * NX + xx)
            for d, xx in enumerate(cross)
        ]

    for part in range(2):
        cols = slice(part * HD, (part + 1) * HD)
        cs[part] = c[:, cols]
        vs[part] = v[:, cols]
    v_pair = pair_copy(vs, vg, 0)
    v_pair.start()
    line_start(cs, cg, 0)
    cg[z] = cs[head]
    vg[head, rows_at(x)] = vs[head]
    v_cross = cross_copies(vg, head, 0)
    for copy in v_cross:
        copy.start()

    reflectors(hh, units, updates, products, lowers, inverses)
    for a in range(2):
        px[x, a] = nn3(products[a, 0], products[a, 1])
    p_cross = [
        send(px.at[x], px.at[x], ps.at[d], pr.at[d], z * NX + xx) for d, xx in enumerate(cross)
    ]
    for copy in p_cross:
        copy.start()

    v_pair.wait()
    v_cross2 = cross_copies(vg, 1 - head, 1)
    for copy in v_cross2:
        copy.start()
    row, col = iotas((HD, HD))
    for a in range(2):
        for b in range(2):
            rows = slice(b * HD, (b + 1) * HD)
            for src, dst in ((q, qlocal), (k, klocal)):
                part = src[rows, a * HD : (a + 1) * HD].astype(F32)
                coef = jnp.where(row >= col, nt3(part, units[a, rows]), 0.0)
                dst[a, rows] = part - nn3(coef, updates[a, rows])

    for copy in p_cross:
        copy.wait()
    for a in range(2):
        one = px[0, a]
        two = nn3(one, px[1, a])
        tz[z, a] = nn3(two, nn3(px[2, a], px[3, a]))
        three = nn3(two, px[2, a])
        totals[a] = jnp.where(
            x == 0, identity(), jnp.where(x == 1, one, jnp.where(x == 2, two, three))
        )
    band = pl.ds(pl.multiple_of(x * 32, 32), 32)

    def t_copy(to, source):
        return send(
            tz.at[source, :, band], tz.at[source, :, band], ts.at[to], tr.at[source], to * NX + x
        )

    def t_forward(source):
        return [
            send(
                tz.at[source, :, band],
                tz.at[source, :, band],
                fs.at[source, d],
                fr.at[source, d],
                z * NX + xx,
            )
            for d, xx in enumerate(cross)
        ]

    def t_start(to, carry):
        t_copy(to, z).start()
        return carry

    lax.fori_loop(z + 1, NZ, t_start, 0)

    def t_step(d, carry):
        @pl.when(d <= z)
        def _():
            t_copy(z, z - d).wait_recv()
            for copy in t_forward(z - d):
                copy.start()

        @pl.when(d > 2)
        def _():
            source = z - d + 2
            for copy in t_forward(source):
                copy.wait()
            for a in range(2):
                totals[a] = nn3(tz[source, a], totals[a])

        return carry

    lax.fori_loop(1, jnp.where(z > 0, z + 3, 1), t_step, 0)
    for a in range(2):
        prefixes[a, 0] = totals[a]
        prefixes[a, 1] = nn3(totals[a], products[a, 0])
        for b in range(2):
            rows = slice(b * HD, (b + 1) * HD)
            ks[a, rows] = nt3(klocal[a, rows], prefixes[a, b]).astype(BF)
    k_pair = pair_copy(ks, kg, 1)
    k_pair.start()
    kg[head, rows_at(x)] = ks[head]
    k_cross = cross_copies(kg, head, 2)
    for copy in k_cross:
        copy.start()
    for a in range(2):
        for b in range(2):
            rows = slice(b * HD, (b + 1) * HD)
            qs[a, rows] = nt3(qlocal[a, rows], prefixes[a, b]).astype(BF)
    line_start(qs, qg, 1)
    qg[z] = qs[head]
    k_pair.wait()
    k_cross2 = cross_copies(kg, 1 - head, 3)
    for copy in k_cross2:
        copy.start()

    def t_done(to, carry):
        t_copy(to, z).wait_send()
        return carry

    lax.fori_loop(z + 1, NZ, t_done, 0)
    for copy in v_cross + v_cross2 + k_cross + k_cross2:
        copy.wait()

    top, total, delta = (held.at[z % 4, i] for i in range(3))
    top[...] = jnp.full(top.shape, LOW, F32)
    total[...] = jnp.zeros(total.shape, F32)
    delta[...] = jnp.zeros(delta.shape, F32)
    key_at, query_at = iotas((ROWS, ROWS))

    def join(at, peak, weight, moment):
        old = top[at, :]
        new = jnp.maximum(old, peak)
        keep, take = jnp.exp2(old - new), jnp.exp2(peak - new)
        top[at, :] = new
        total[at, :] = total[at, :] * keep + weight * take
        delta[at, :] = delta[at, :] * keep + moment * take

    def forward_full(r, slot):
        query, cot = qg[r], cg[r]
        peak = None
        for j in range(NX):
            rows = slice(j * ROWS, (j + 1) * ROWS)
            score = nt(kg[slot, rows], query) * SCALE2
            s_scr[rows] = score
            high = jnp.max(score, axis=0, keepdims=True)
            peak = high if peak is None else jnp.maximum(peak, high)
        weight = moment = jnp.zeros((1, ROWS), F32)
        for j in range(NX):
            rows = slice(j * ROWS, (j + 1) * ROWS)
            p = jnp.exp2(s_scr[rows] - peak)
            weight = weight + jnp.sum(p, axis=0, keepdims=True)
            moment = moment + jnp.sum(p * nt(vg[slot, rows], cot), axis=0, keepdims=True)
        join(pl.ds(r, 1), peak, weight, moment)

    def forward_edge(r, slot):
        def step(j, carry):
            rows = rows_at(j)
            live = key_at + j * ROWS <= query_at + x * ROWS
            score = jnp.where(live, nt(kg[slot, rows], qg[r]) * SCALE2, LOW)
            peak = jnp.max(score, axis=0, keepdims=True)
            p = jnp.where(live, jnp.exp2(score - peak), 0.0)
            moment = jnp.sum(p * nt(vg[slot, rows], cg[r]), axis=0, keepdims=True)
            join(pl.ds(r, 1), peak, jnp.sum(p, axis=0, keepdims=True), moment)
            return carry

        lax.fori_loop(0, x + 1, step, 0)

    def forward_row(n, carry):
        offset = (n + 1) // 2
        r = (z + NZ + jnp.where(n % 2 == 1, offset, -offset)) % NZ

        @pl.when((r != z) & (r >= low_row))
        def _():
            line_copy(cs, cg, 0, z, r).wait_recv()
            line_copy(qs, qg, 1, z, r).wait_recv()

        def slot_step(slot, carry):
            key_row = jnp.where(slot == 0, low_row, NZ - 1 - low_row)

            @pl.when(r > key_row)
            def _():
                forward_full(r, slot)

            @pl.when(r == key_row)
            def _():
                forward_edge(r, slot)

            return carry

        return lax.fori_loop(0, 2, slot_step, carry)

    lax.fori_loop(0, NZ, forward_row, 0)

    half_peers = [(head * 4 + (z + d) % 4) * NX + x for d in range(1, 4)]
    stat_copies = [
        send(held.at[z % 4], held.at[z % 4], ss.at[d], sr.at[d], peer)
        for d, peer in enumerate(half_peers)
    ]
    for copy in stat_copies:
        copy.start()
    line_wait_send(cs, cg, 0)
    line_wait_send(qs, qg, 1)
    dq_acc[...] = jnp.zeros(dq_acc.shape, F32)
    dk_acc[...] = jnp.zeros(dk_acc.shape, F32)
    dv_acc[...] = jnp.zeros(dv_acc.shape, F32)
    for slot in range(2):
        for j in range(NX):
            kt[slot, j] = kg[slot, j * ROWS : (j + 1) * ROWS].T
    for copy in stat_copies:
        copy.wait()
    peak = held[0, 0]
    for i in range(1, 4):
        peak = jnp.maximum(peak, held[i, 0])
    weight = moment = jnp.zeros(peak.shape, F32)
    for i in range(4):
        take = jnp.exp2(held[i, 0] - peak)
        weight = weight + held[i, 1] * take
        moment = moment + held[i, 2] * take
    log_total[...] = peak + jnp.log2(weight)
    delta_row[...] = moment / weight

    def tile(r, slot, j, rows, live):
        key, query, cot = kg[slot, rows], qg[r], cg[r]
        at = pl.ds(r, 1)
        score = nt(key, query) * SCALE2 - log_total[at, :]
        if live is not None:
            score = jnp.where(live, score, LOW)
        p = jnp.exp2(score)
        grad = (p * (nt(vg[slot, rows], cot) - delta_row[at, :])).astype(BF)
        dv_acc[slot, rows] += nn(p.astype(BF), cot)
        dk_acc[slot, rows] += nn(grad, query)
        return nn(kt[slot, j], grad)

    def backward_full(r, slot):
        total = None
        for j in range(NX):
            part = tile(r, slot, j, slice(j * ROWS, (j + 1) * ROWS), None)
            total = part if total is None else total + part
        dq_acc[r] += total

    def backward_edge(r, slot):
        def step(j, carry):
            live = key_at + j * ROWS <= query_at + x * ROWS
            dq_acc[r] += tile(r, slot, j, rows_at(j), live)
            return carry

        lax.fori_loop(0, x + 1, step, 0)

    def dq_copy(to, source):
        return send(dqt.at[to], rq.at[source], zs.at[2, to], zr.at[2, source], to * NX + x)

    def backward_row(n, carry):
        slot = jnp.where(n < NZ, 1 - head, head)
        key_row = jnp.where(slot == 0, low_row, NZ - 1 - low_row)
        m = n % NZ
        offset = 4 - (m + 1) // 2
        r = (z + NZ + jnp.where(m % 2 == 1, offset, -offset)) % NZ

        @pl.when(r > key_row)
        def _():
            backward_full(r, slot)

        @pl.when(r == key_row)
        def _():
            backward_edge(r, slot)

        @pl.when((n >= NZ) & (r >= low_row))
        def _():
            dqt[r] = (dq_acc[r] * SCALE).astype(BF)

            @pl.when(r != z)
            def _():
                dq_copy(r, z).start()

        @pl.when((n == NZ - 1) | (n == 2 * NZ - 1))
        def _():
            i = n // NZ
            dkv[slot, :, :HD] = (dk_acc[slot] * SCALE).astype(BF)
            dkv[slot, :, HD:] = dv_acc[slot].astype(BF)
            rx[x, i] = dkv[slot, rows_at(x)]
            for copy in kv_copies(i):
                copy.start()

        return carry

    def kv_copies(i):
        slot = jnp.where(i == 0, 1 - head, head)
        return [
            send(dkv.at[slot, rows_at(xx)], rx.at[x, i], xs.at[4 + i, d], xr.at[4 + i, d], z * NX + xx)
            for d, xx in enumerate(cross)
        ]

    lax.fori_loop(0, 2 * NZ, backward_row, 0)

    def summed(i):
        return (rx[0, i].astype(F32) + rx[1, i].astype(F32)) + (
            rx[2, i].astype(F32) + rx[3, i].astype(F32)
        )

    for copy in kv_copies(0):
        copy.wait()
    pair_out[0] = summed(0).astype(BF)
    pair = send(pair_out.at[0], pair_out.at[1], os.at[2], orr.at[2], other * NX + x)
    pair.start()

    rq[z] = dqt[z]

    def dq_wait(d, carry):
        to = (z + d) % NZ

        @pl.when(to >= low_row)
        def _():
            dq_copy(to, z).wait_send()

        @pl.when(z >= jnp.minimum(to, NZ - 1 - to))
        def _():
            dq_copy(z, to).wait_recv()

        @pl.when(z < jnp.minimum(to, NZ - 1 - to))
        def _():
            rq[to] = jnp.zeros(rq.shape[1:], BF)

        return carry

    lax.fori_loop(1, NZ, dq_wait, 0)

    def turn_back(i, a, b, part):
        rows, cols = slice(b * HD, (b + 1) * HD), slice(a * HD, (a + 1) * HD)
        back = nn3(part, prefixes[a, b])
        coef = jnp.where(row >= col, nt3(back, updates[a, rows]), 0.0)
        grads[i, rows, cols] = (back - nn3(coef, units[a, rows])).astype(BF)

    for a in range(2):
        total = rq[4 * a].astype(F32)
        for i in range(1, 4):
            total = total + rq[4 * a + i].astype(F32)
        total = total.T
        for b in range(2):
            turn_back(0, a, b, total[b * HD : (b + 1) * HD])
    for copy in kv_copies(1):
        copy.wait()
    kv[head] = summed(1)
    pair.wait()
    kv[1 - head] = pair_out[1].astype(F32)
    for a in range(2):
        grads[2, :, a * HD : (a + 1) * HD] = kv[a, :, HD:].astype(BF)
        for b in range(2):
            turn_back(1, a, b, kv[a, b * HD : (b + 1) * HD, :HD])
    for load in loads:
        load.wait()

    def columns(block):
        at = pl.ds(pl.multiple_of(block * 512, 512), 512)
        return (
            nt(grads[0], w[0, at, :]) + nt(grads[1], w[1, at, :]) + nt(grads[2], w[2, at, :])
        )

    blocks = order + [y]
    swaps, hops = [], []

    def give(i):
        mine[i] = columns(blocks[i] * 2 + 1 - core).astype(BF)
        swap = send(mine.at[i], theirs.at[i], ms.at[i], mr.at[i], mate, "head")
        swap.start()
        swaps.append(swap)

    give(0)
    give(1)
    for i, yy in enumerate(blocks):
        part = columns(yy * 2 + core)
        if i + 2 < 4:
            give(i + 2)
        swaps[i].wait()
        part = part + theirs[i].astype(F32)
        if i < 3:
            relay[i] = part.astype(BF)
            hop = send(relay.at[i], landed.at[i], ys.at[i], yr.at[i], yy * 2 + core, "head")
            hop.start()
            hops.append(hop)
        else:
            out[...] = part
    for hop in hops:
        hop.wait()
    out[...] = (out[...] + landed[0].astype(F32)) + (
        landed[1].astype(F32) + landed[2].astype(F32)
    )


def on_device(query, key, value, householder, cotangent, w_query, w_key, w_value):
    dma = pltpu.SemaphoreType.DMA
    own, own32 = ((2, ROWS, HD), BF), ((2, ROWS, HD), F32)
    lines, keys = ((NZ, ROWS, HD), BF), ((2, NX * ROWS, HD), BF)
    square = (HD, HD)
    stat = ((NZ, ROWS), F32)
    acc = ((2, NX * ROWS, HD), F32)
    block = (ROWS, 2 * HD)
    wide = (ROWS, 512)
    scratch = [
        lines, lines, keys, keys, own32, own32, ((2, 2) + square, F32),
        own, own, own, own, ((NX, 2) + square, F32), ((NZ, 2) + square, F32), own32, own32,
        ((2, 2) + square, F32), ((4,) + square, F32), ((4,) + square, F32), ((2,) + square, F32),
        ((NX * ROWS, ROWS), F32), ((4, 3, NZ, ROWS), F32), stat, stat,
        ((2, NX, HD, ROWS), BF), ((NZ, HD, ROWS), F32), acc, acc,
        ((NZ, HD, ROWS), BF), ((2, NX * ROWS, 2 * HD), BF), ((NZ, HD, ROWS), BF),
        ((NX, 2) + block, BF), ((2,) + block, BF), ((2,) + block, F32),
        ((3, 4096, ROWS), BF), ((3,) + block, BF),
        ((4,) + wide, BF), ((4,) + wide, BF), ((3,) + wide, BF), ((3,) + wide, BF),
    ]
    sems = [
        (3, 8), (3, 8), (6, 3), (6, 3), (3,), (3,), (8,), (8,), (8, 3), (8, 3), (3,), (3,),
        (3,), (3,), (3,), (4,), (4,), (3,), (3,),
    ]
    vmem = pl.BlockSpec(memory_space=pltpu.VMEM)
    return pl.pallas_call(
        whole_kernel,
        out_shape=jax.ShapeDtypeStruct(wide, F32),
        in_specs=[vmem] * 5 + [pl.BlockSpec(memory_space=pl.ANY)] * 3,
        out_specs=vmem,
        scratch_shapes=[pltpu.VMEM(*s) for s in scratch] + [dma(s) for s in sems],
        compiler_params=pltpu.CompilerParams(
            vmem_limit_bytes=VMEM_BYTES, collective_id=0, has_side_effects=True
        ),
    )(householder, query, key, value, cotangent, w_query, w_key, w_value)


def solution(mesh):
    return jax.shard_map(
        on_device,
        mesh=mesh,
        in_specs=(P("ctx", "head"),) * 5 + (P(None, "head"),) * 3,
        out_specs=P("ctx", "head"),
        check_vma=False,
    )
```

time: 155 us -> 104 us (0.67)
  Pallas kernels: 152 us -> 102 us
    pallas_call x6 -> x1, Pallas kernels: 152 us -> 102 us  [on_device(): pl.pallas_call(whole_kernel, out_shape=jax.ShapeDtypeStruct(wide, F32), i...]
where the time goes in v2:
time: 104 us
  Pallas kernels  102 us (98%)
  local copies, waits for them, and re-layouts  1.87 us (2%)
    pallas_call x1, Pallas kernels, on_device(): pl.pallas_call(whole_kernel, out_shape=jax.ShapeDtypeStruct(wide, F32), i...  102 us

profile of v2, /device:TPU:1, one launch (start us, length us, event | category | flops | bytes accessed | tf_op | source)
XLA Modules:
  0.0 103.8 jit_solution(10678416586282560950)
XLA Ops:
  0.0 101.9 %shard_map.82 = f32[256,512]{1,0:T(8,128)} custom-call(bf16[256,256]{1,0:T(8,128)(2,1)} %hh.1, bf16[256,256]{1,0:T(8,128)(2,1)} %q.1, bf16[256,256]{1,0:T(8,128)(2,1)} %k.1, bf16[256,256]{1,0:T(8,128)(2,1)} %v.1, bf16[256,256]{1,0:T(8,128)(2,1)} %c.1, bf16[4096,256]{1,0:T(8,128)(2,1)} %wq.1, bf16[4096,256]{1,0:T(8,128)(2,1)} %wk.1, bf16[4096,256]{1,0:T(8,128)(2,1)} %wv.1), custom_call_target="tpu_custom_call" | custom-call | tf_op jit(solution)/shard_map/pallas_call | solution.py:581
  102.0 1.9 %copy.10 = f32[256,512]{1,0:T(8,128)} copy(f32[256,512]{1,0:T(8,128)} %shard_map.82) | data formatting | bytes 1048576

commit v3 on v2

--- a/solution.py
+++ b/solution.py
@@ -44,6 +44,11 @@
     return nt(ah, bh) + (nt(al, bh) + nt(ah, bl))
 
 
+def nn2(a, b):
+    bh, bl = split(b)
+    return nn(a, bh) + nn(a, bl)
+
+
 def iotas(shape):
     return lax.broadcasted_iota(jnp.int32, shape, 0), lax.broadcasted_iota(jnp.int32, shape, 1)
 
@@ -102,14 +107,14 @@
 
 
 def whole_kernel(
-    hh, q, k, v, c, wq, wk, wv,
+    hh_in, q_in, k_in, v_in, c_in, wq, wk, wv,
     out,
-    qg, cg, kg, vg, units, updates, prefixes,
+    hh, q, k, v, c, qg, cg, kg, vg, units, updates, prefixes,
     qs, ks, cs, vs, px, tz, qlocal, klocal, products, lowers, inverses, totals,
     s_scr, held, log_total, delta_row,
     kt, dq_acc, dk_acc, dv_acc, dqt, dkv, rq, rx, pair_out, kv,
-    w, grads, mine, theirs, relay, landed,
-    zs, zr, xs, xr, ps, pr, ts, tr, fs, fr, os, orr, ss, sr, ws, ms, mr, ys, yr,
+    w, grads, mine, theirs, relay, landed, joined,
+    zs, zr, xs, xr, ps, pr, ts, tr, fs, fr, os, orr, ss, sr, ws, ins, ms, mr, ys, yr,
 ):
     z, x = place()
     me = lax.axis_index("head")
@@ -120,13 +125,14 @@
     other = NZ - 1 - z
     line = [(z + d) % NZ for d in range(1, NZ)]
     cross = [(x + d) % NX for d in range(1, NX)]
-    order = [(y + d) % 4 for d in (2, 1, 3)]
-    loads = [pltpu.make_async_copy(src, w.at[i], ws.at[i]) for i, src in enumerate((wq, wk, wv))]
-    for load in loads:
-        load.start()
+    above, below = (y + 1) % 4, (y + 3) % 4
+    pairs = ((c_in, c), (v_in, v), (hh_in, hh), (q_in, q), (k_in, k))
+    reads = [pltpu.make_async_copy(src, dst, ins.at[i]) for i, (src, dst) in enumerate(pairs)]
+    for read in reads:
+        read.start()
     barrier = pltpu.get_barrier_semaphore()
     peers = [{"ctx": zz * NX + x} for zz in line] + [{"ctx": z * NX + xx} for xx in cross]
-    peers = peers + [{"head": mate}] + [{"head": yy * 2 + core} for yy in order]
+    peers = peers + [{"head": mate}] + [{"head": yy * 2 + core} for yy in (above, below)]
     for peer in peers:
         pl.semaphore_signal(barrier, inc=1, device_id=peer, device_id_type=MESH)
     pl.semaphore_wait(barrier, len(peers))
@@ -169,6 +175,8 @@
             for d, xx in enumerate(cross)
         ]
 
+    for read in reads:
+        read.wait()
     for part in range(2):
         cols = slice(part * HD, (part + 1) * HD)
         cs[part] = c[:, cols]
@@ -181,6 +189,9 @@
     v_cross = cross_copies(vg, head, 0)
     for copy in v_cross:
         copy.start()
+    loads = [pltpu.make_async_copy(src, w.at[i], ws.at[i]) for i, src in enumerate((wq, wk, wv))]
+    for load in loads:
+        load.start()
 
     reflectors(hh, units, updates, products, lowers, inverses)
     for a in range(2):
@@ -209,7 +220,7 @@
     for a in range(2):
         one = px[0, a]
         two = nn3(one, px[1, a])
-        tz[z, a] = nn3(two, nn3(px[2, a], px[3, a]))
+        tz[z, a] = nn3(two, nn3(px[2, a], px[3, a])).astype(BF)
         three = nn3(two, px[2, a])
         totals[a] = jnp.where(
             x == 0, identity(), jnp.where(x == 1, one, jnp.where(x == 2, two, three))
@@ -252,7 +263,7 @@
             for copy in t_forward(source):
                 copy.wait()
             for a in range(2):
-                totals[a] = nn3(tz[source, a], totals[a])
+                totals[a] = nn2(tz[source, a], totals[a])
 
         return carry
 
@@ -285,7 +296,7 @@
         return carry
 
     lax.fori_loop(z + 1, NZ, t_done, 0)
-    for copy in v_cross + v_cross2 + k_cross + k_cross2:
+    for copy in v_cross + v_cross2 + k_cross:
         copy.wait()
 
     top, total, delta = (held.at[z % 4, i] for i in range(3))
@@ -333,30 +344,33 @@
         lax.fori_loop(0, x + 1, step, 0)
 
     def forward_row(n, carry):
-        offset = (n + 1) // 2
-        r = (z + NZ + jnp.where(n % 2 == 1, offset, -offset)) % NZ
-
-        @pl.when((r != z) & (r >= low_row))
+        slot = jnp.where(n < NZ, head, 1 - head)
+        key_row = jnp.where(slot == 0, low_row, NZ - 1 - low_row)
+        m = n % NZ
+        offset = (m + 1) // 2
+        r = (z + NZ + jnp.where(m % 2 == 1, offset, -offset)) % NZ
+
+        @pl.when((n < NZ) & (r != z) & (r >= low_row))
         def _():
             line_copy(cs, cg, 0, z, r).wait_recv()
             line_copy(qs, qg, 1, z, r).wait_recv()
 
-        def slot_step(slot, carry):
-            key_row = jnp.where(slot == 0, low_row, NZ - 1 - low_row)
-
-            @pl.when(r > key_row)
-            def _():
-                forward_full(r, slot)
-
-            @pl.when(r == key_row)
-            def _():
-                forward_edge(r, slot)
-
-            return carry
-
-        return lax.fori_loop(0, 2, slot_step, carry)
-
-    lax.fori_loop(0, NZ, forward_row, 0)
+        @pl.when(n == NZ)
+        def _():
+            for copy in k_cross2:
+                copy.wait()
+
+        @pl.when(r > key_row)
+        def _():
+            forward_full(r, slot)
+
+        @pl.when(r == key_row)
+        def _():
+            forward_edge(r, slot)
+
+        return carry
+
+    lax.fori_loop(0, 2 * NZ, forward_row, 0)
 
     half_peers = [(head * 4 + (z + d) % 4) * NX + x for d in range(1, 4)]
     stat_copies = [
@@ -492,7 +506,7 @@
     lax.fori_loop(1, NZ, dq_wait, 0)
 
     def turn_back(i, a, b, part):
-        rows, cols = slice(b * HD, (b + 1) * HD), slice(a * HD, (a + 1) * HD)
+        rows, cols = slice(b * HD, (b + 1) * HD), pl.ds(pl.multiple_of(a * HD, HD), HD)
         back = nn3(part, prefixes[a, b])
         coef = jnp.where(row >= col, nt3(back, updates[a, rows]), 0.0)
         grads[i, rows, cols] = (back - nn3(coef, units[a, rows])).astype(BF)
@@ -506,13 +520,17 @@
             turn_back(0, a, b, total[b * HD : (b + 1) * HD])
     for copy in kv_copies(1):
         copy.wait()
+
+    def finish(a):
+        grads[2, :, pl.ds(pl.multiple_of(a * HD, HD), HD)] = kv[a, :, HD:].astype(BF)
+        for b in range(2):
+            turn_back(1, a, b, kv[a, b * HD : (b + 1) * HD, :HD])
+
     kv[head] = summed(1)
+    finish(head)
     pair.wait()
     kv[1 - head] = pair_out[1].astype(F32)
-    for a in range(2):
-        grads[2, :, a * HD : (a + 1) * HD] = kv[a, :, HD:].astype(BF)
-        for b in range(2):
-            turn_back(1, a, b, kv[a, b * HD : (b + 1) * HD, :HD])
+    finish(1 - head)
     for load in loads:
         load.wait()
 
@@ -522,8 +540,9 @@
             nt(grads[0], w[0, at, :]) + nt(grads[1], w[1, at, :]) + nt(grads[2], w[2, at, :])
         )
 
-    blocks = order + [y]
-    swaps, hops = [], []
+    half = ROWS // 2
+    blocks = [(y + 2) % 4, above, below, y]
+    swaps = []
 
     def give(i):
         mine[i] = columns(blocks[i] * 2 + 1 - core).astype(BF)
@@ -531,26 +550,41 @@
         swap.start()
         swaps.append(swap)
 
+    def take(i):
+        part = columns(blocks[i] * 2 + core)
+        swaps[i].wait()
+        return part + theirs[i].astype(F32)
+
+    def hop(i, src, dst, to):
+        copy = send(src, dst, ys.at[i], yr.at[i], to * 2 + core, "head")
+        copy.start()
+        return copy
+
     give(0)
     give(1)
-    for i, yy in enumerate(blocks):
-        part = columns(yy * 2 + core)
-        if i + 2 < 4:
-            give(i + 2)
-        swaps[i].wait()
-        part = part + theirs[i].astype(F32)
-        if i < 3:
-            relay[i] = part.astype(BF)
-            hop = send(relay.at[i], landed.at[i], ys.at[i], yr.at[i], yy * 2 + core, "head")
-            hop.start()
-            hops.append(hop)
-        else:
-            out[...] = part
-    for hop in hops:
-        hop.wait()
-    out[...] = (out[...] + landed[0].astype(F32)) + (
-        landed[1].astype(F32) + landed[2].astype(F32)
-    )
+    relay[0] = take(0).astype(BF)
+    up = hop(0, relay.at[0, :half], landed.at[0, :half], above)
+    down = hop(1, relay.at[0, half:], landed.at[0, half:], below)
+    give(2)
+    part = take(1)
+    joined[0] = part[:half]
+    relay[1, half:] = part[half:].astype(BF)
+    hops = [hop(2, relay.at[1, half:], landed.at[1, half:], above)]
+    give(3)
+    part = take(2)
+    joined[1] = part[half:]
+    relay[2, :half] = part[:half].astype(BF)
+    hops.append(hop(3, relay.at[2, :half], landed.at[2, :half], below))
+    up.wait()
+    relay[1, :half] = (joined[0] + landed[0, :half].astype(F32)).astype(BF)
+    hops.append(hop(4, relay.at[1, :half], landed.at[1, :half], above))
+    down.wait()
+    relay[2, half:] = (joined[1] + landed[0, half:].astype(F32)).astype(BF)
+    hops.append(hop(5, relay.at[2, half:], landed.at[2, half:], below))
+    out[...] = take(3)
+    for copy in hops:
+        copy.wait()
+    out[...] = out[...] + (landed[1].astype(F32) + landed[2].astype(F32))
 
 
 def on_device(query, key, value, householder, cotangent, w_query, w_key, w_value):
@@ -562,9 +596,9 @@
     acc = ((2, NX * ROWS, HD), F32)
     block = (ROWS, 2 * HD)
     wide = (ROWS, 512)
-    scratch = [
+    scratch = [(block, BF)] * 5 + [
         lines, lines, keys, keys, own32, own32, ((2, 2) + square, F32),
-        own, own, own, own, ((NX, 2) + square, F32), ((NZ, 2) + square, F32), own32, own32,
+        own, own, own, own, ((NX, 2) + square, F32), ((NZ, 2) + square, BF), own32, own32,
         ((2, 2) + square, F32), ((4,) + square, F32), ((4,) + square, F32), ((2,) + square, F32),
         ((NX * ROWS, ROWS), F32), ((4, 3, NZ, ROWS), F32), stat, stat,
         ((2, NX, HD, ROWS), BF), ((NZ, HD, ROWS), F32), acc, acc,
@@ -572,16 +606,17 @@
         ((NX, 2) + block, BF), ((2,) + block, BF), ((2,) + block, F32),
         ((3, 4096, ROWS), BF), ((3,) + block, BF),
         ((4,) + wide, BF), ((4,) + wide, BF), ((3,) + wide, BF), ((3,) + wide, BF),
+        ((2, ROWS // 2, 512), F32),
     ]
     sems = [
         (3, 8), (3, 8), (6, 3), (6, 3), (3,), (3,), (8,), (8,), (8, 3), (8, 3), (3,), (3,),
-        (3,), (3,), (3,), (4,), (4,), (3,), (3,),
+        (3,), (3,), (3,), (5,), (4,), (4,), (6,), (6,),
     ]
     vmem = pl.BlockSpec(memory_space=pltpu.VMEM)
     return pl.pallas_call(
         whole_kernel,
         out_shape=jax.ShapeDtypeStruct(wide, F32),
-        in_specs=[vmem] * 5 + [pl.BlockSpec(memory_space=pl.ANY)] * 3,
+        in_specs=[pl.BlockSpec(memory_space=pl.ANY)] * 8,
         out_specs=vmem,
         scratch_shapes=[pltpu.VMEM(*s) for s in scratch] + [dma(s) for s in sems],
         compiler_params=pltpu.CompilerParams(

time: 104 us -> 96.4 us (0.927)
  Pallas kernels: 102 us -> 94 us
    pallas_call x1, Pallas kernels: 102 us -> 94 us  [on_device(): pl.pallas_call(whole_kernel, out_shape=jax.ShapeDtypeStruct(wide, F32), i...]
where the time goes in v3:
time: 96.4 us; the launch traced here: 95.9 us
  Pallas kernels  94 us (98%)
  local copies, waits for them, and re-layouts  1.87 us (2%)
    pallas_call x1, Pallas kernels, on_device(): pl.pallas_call(whole_kernel, out_shape=jax.ShapeDtypeStruct(wide, F32), i...  94 us

profile of v3, /device:TPU:1, one launch (start us, length us, event | category | flops | bytes accessed | tf_op | source)
XLA Modules:
  0.0 95.9 jit_solution(6748796962493841787)
XLA Ops:
  0.0 94.0 %shard_map.82 = f32[256,512]{1,0:T(8,128)} custom-call(bf16[256,256]{1,0:T(8,128)(2,1)} %hh_in.1, bf16[256,256]{1,0:T(8,128)(2,1)} %q_in.1, bf16[256,256]{1,0:T(8,128)(2,1)} %k_in.1, bf16[256,256]{1,0:T(8,128)(2,1)} %v_in.1, bf16[256,256]{1,0:T(8,128)(2,1)} %c_in.1, bf16[4096,256]{1,0:T(8,128)(2,1)} %wq.1, bf16[4096,256]{1,0:T(8,128)(2,1)} %wk.1, ...), custom_call_target="tpu_custom_call" | custom-call | tf_op jit(solution)/shard_map/pallas_call | solution.py:616
  94.0 1.9 %copy.10 = f32[256,512]{1,0:T(8,128)} copy(f32[256,512]{1,0:T(8,128)} %shard_map.82) | data formatting | bytes 1048576

commit v4 on v3

--- a/solution.py
+++ b/solution.py
@@ -111,7 +111,7 @@
     out,
     hh, q, k, v, c, qg, cg, kg, vg, units, updates, prefixes,
     qs, ks, cs, vs, px, tz, qlocal, klocal, products, lowers, inverses, totals,
-    s_scr, held, log_total, delta_row,
+    gw, pt, peaks, held, log_total, delta_row,
     kt, dq_acc, dk_acc, dv_acc, dqt, dkv, rq, rx, pair_out, kv,
     w, grads, mine, theirs, relay, landed, joined,
     zs, zr, xs, xr, ps, pr, ts, tr, fs, fr, os, orr, ss, sr, ws, ins, ms, mr, ys, yr,
@@ -286,6 +286,30 @@
             qs[a, rows] = nt3(qlocal[a, rows], prefixes[a, b]).astype(BF)
     line_start(qs, qg, 1)
     qg[z] = qs[head]
+    for copy in v_cross + v_cross2:
+        copy.wait()
+
+    def c_wait(d, carry):
+        source = (z + d) % NZ
+
+        @pl.when(source >= low_row)
+        def _():
+            line_copy(cs, cg, 0, z, source).wait_recv()
+
+        return carry
+
+    lax.fori_loop(1, NZ, c_wait, 0)
+
+    def weigh(t, carry):
+        slot = jnp.where(t < NZ - low_row, 0, 1)
+        r = jnp.where(slot == 0, t + low_row, t - 1)
+        cot = cg[r]
+        for j in range(NX):
+            rows = slice(j * ROWS, (j + 1) * ROWS)
+            gw[t, rows] = nt(vg[slot, rows], cot)
+        return carry
+
+    lax.fori_loop(0, 9, weigh, 0)
     k_pair.wait()
     k_cross2 = cross_copies(kg, 1 - head, 3)
     for copy in k_cross2:
@@ -296,7 +320,7 @@
         return carry
 
     lax.fori_loop(z + 1, NZ, t_done, 0)
-    for copy in v_cross + v_cross2 + k_cross:
+    for copy in k_cross:
         copy.wait()
 
     top, total, delta = (held.at[z % 4, i] for i in range(3))
@@ -313,35 +337,52 @@
         total[at, :] = total[at, :] * keep + weight * take
         delta[at, :] = delta[at, :] * keep + moment * take
 
+    def tile_of(r, slot):
+        return jnp.where(slot == 0, r - low_row, r + 1)
+
     def forward_full(r, slot):
-        query, cot = qg[r], cg[r]
+        query, t = qg[r], tile_of(r, slot)
         peak = None
         for j in range(NX):
             rows = slice(j * ROWS, (j + 1) * ROWS)
             score = nt(kg[slot, rows], query) * SCALE2
-            s_scr[rows] = score
+            pt[t, rows] = score
             high = jnp.max(score, axis=0, keepdims=True)
             peak = high if peak is None else jnp.maximum(peak, high)
         weight = moment = jnp.zeros((1, ROWS), F32)
         for j in range(NX):
             rows = slice(j * ROWS, (j + 1) * ROWS)
-            p = jnp.exp2(s_scr[rows] - peak)
+            p = jnp.exp2(pt[t, rows] - peak)
+            pt[t, rows] = p
             weight = weight + jnp.sum(p, axis=0, keepdims=True)
-            moment = moment + jnp.sum(p * nt(vg[slot, rows], cot), axis=0, keepdims=True)
+            moment = moment + jnp.sum(p * gw[t, rows], axis=0, keepdims=True)
+        peaks[pl.ds(t, 1), :] = peak
         join(pl.ds(r, 1), peak, weight, moment)
 
     def forward_edge(r, slot):
-        def step(j, carry):
+        t = tile_of(r, slot)
+
+        def scores(j, peak):
             rows = rows_at(j)
             live = key_at + j * ROWS <= query_at + x * ROWS
             score = jnp.where(live, nt(kg[slot, rows], qg[r]) * SCALE2, LOW)
-            peak = jnp.max(score, axis=0, keepdims=True)
-            p = jnp.where(live, jnp.exp2(score - peak), 0.0)
-            moment = jnp.sum(p * nt(vg[slot, rows], cg[r]), axis=0, keepdims=True)
-            join(pl.ds(r, 1), peak, jnp.sum(p, axis=0, keepdims=True), moment)
-            return carry
-
-        lax.fori_loop(0, x + 1, step, 0)
+            pt[t, rows] = score
+            return jnp.maximum(peak, jnp.max(score, axis=0, keepdims=True))
+
+        peak = lax.fori_loop(0, x + 1, scores, jnp.full((1, ROWS), LOW, F32))
+
+        def sums(j, carry):
+            weight, moment = carry
+            rows = rows_at(j)
+            p = jnp.exp2(pt[t, rows] - peak)
+            pt[t, rows] = p
+            weight = weight + jnp.sum(p, axis=0, keepdims=True)
+            return weight, moment + jnp.sum(p * gw[t, rows], axis=0, keepdims=True)
+
+        nothing = jnp.zeros((1, ROWS), F32)
+        weight, moment = lax.fori_loop(0, x + 1, sums, (nothing, nothing))
+        peaks[pl.ds(t, 1), :] = peak
+        join(pl.ds(r, 1), peak, weight, moment)
 
     def forward_row(n, carry):
         slot = jnp.where(n < NZ, head, 1 - head)
@@ -352,7 +393,6 @@
 
         @pl.when((n < NZ) & (r != z) & (r >= low_row))
         def _():
-            line_copy(cs, cg, 0, z, r).wait_recv()
             line_copy(qs, qg, 1, z, r).wait_recv()
 
         @pl.when(n == NZ)
@@ -400,29 +440,24 @@
     log_total[...] = peak + jnp.log2(weight)
     delta_row[...] = moment / weight
 
-    def tile(r, slot, j, rows, live):
-        key, query, cot = kg[slot, rows], qg[r], cg[r]
-        at = pl.ds(r, 1)
-        score = nt(key, query) * SCALE2 - log_total[at, :]
-        if live is not None:
-            score = jnp.where(live, score, LOW)
-        p = jnp.exp2(score)
-        grad = (p * (nt(vg[slot, rows], cot) - delta_row[at, :])).astype(BF)
-        dv_acc[slot, rows] += nn(p.astype(BF), cot)
-        dk_acc[slot, rows] += nn(grad, query)
+    def tile(r, slot, j, rows):
+        t, at = tile_of(r, slot), pl.ds(r, 1)
+        p = pt[t, rows] * jnp.exp2(peaks[pl.ds(t, 1), :] - log_total[at, :])
+        grad = (p * (gw[t, rows] - delta_row[at, :])).astype(BF)
+        dv_acc[slot, rows] += nn(p.astype(BF), cg[r])
+        dk_acc[slot, rows] += nn(grad, qg[r])
         return nn(kt[slot, j], grad)
 
     def backward_full(r, slot):
         total = None
         for j in range(NX):
-            part = tile(r, slot, j, slice(j * ROWS, (j + 1) * ROWS), None)
+            part = tile(r, slot, j, slice(j * ROWS, (j + 1) * ROWS))
             total = part if total is None else total + part
         dq_acc[r] += total
 
     def backward_edge(r, slot):
         def step(j, carry):
-            live = key_at + j * ROWS <= query_at + x * ROWS
-            dq_acc[r] += tile(r, slot, j, rows_at(j), live)
+            dq_acc[r] += tile(r, slot, j, rows_at(j))
             return carry
 
         lax.fori_loop(0, x + 1, step, 0)
@@ -445,7 +480,9 @@
         def _():
             backward_edge(r, slot)
 
-        @pl.when((n >= NZ) & (r >= low_row))
+        alone = (head == 1) & (r < NZ - 1 - low_row)
+
+        @pl.when((r >= low_row) & ((n >= NZ) != alone))
         def _():
             dqt[r] = (dq_acc[r] * SCALE).astype(BF)
 
@@ -600,7 +637,7 @@
         lines, lines, keys, keys, own32, own32, ((2, 2) + square, F32),
         own, own, own, own, ((NX, 2) + square, F32), ((NZ, 2) + square, BF), own32, own32,
         ((2, 2) + square, F32), ((4,) + square, F32), ((4,) + square, F32), ((2,) + square, F32),
-        ((NX * ROWS, ROWS), F32), ((4, 3, NZ, ROWS), F32), stat, stat,
+        ((9, NX * ROWS, ROWS), F32), ((9, NX * ROWS, ROWS), F32), ((16, ROWS), F32), ((4, 3, NZ, ROWS), F32), stat, stat,
         ((2, NX, HD, ROWS), BF), ((NZ, HD, ROWS), F32), acc, acc,
         ((NZ, HD, ROWS), BF), ((2, NX * ROWS, 2 * HD), BF), ((NZ, HD, ROWS), BF),
         ((NX, 2) + block, BF), ((2,) + block, BF), ((2,) + block, F32),

time: 96.4 us -> 93.4 us (0.969)
  Pallas kernels: 94 us -> 90.7 us
    pallas_call x1, Pallas kernels: 94 us -> 90.7 us  [on_device(): pl.pallas_call(whole_kernel, out_shape=jax.ShapeDtypeStruct(wide, F32), i...]
where the time goes in v4:
time: 93.4 us; the launch traced here: 92.6 us
  Pallas kernels  90.7 us (97%)
  local copies, waits for them, and re-layouts  1.87 us (2%)
    pallas_call x1, Pallas kernels, on_device(): pl.pallas_call(whole_kernel, out_shape=jax.ShapeDtypeStruct(wide, F32), i...  90.7 us
    unnamed x1, local copies, waits for them, and re-layouts  1.87 us

profile of v4, /device:TPU:1, one launch (start us, length us, event | category | flops | bytes accessed | tf_op | source)
XLA Modules:
  0.0 92.6 jit_solution(14340610212893167732)
XLA Ops:
  0.0 90.7 %shard_map.82 = f32[256,512]{1,0:T(8,128)} custom-call(bf16[256,256]{1,0:T(8,128)(2,1)} %hh_in.1, bf16[256,256]{1,0:T(8,128)(2,1)} %q_in.1, bf16[256,256]{1,0:T(8,128)(2,1)} %k_in.1, bf16[256,256]{1,0:T(8,128)(2,1)} %v_in.1, bf16[256,256]{1,0:T(8,128)(2,1)} %c_in.1, bf16[4096,256]{1,0:T(8,128)(2,1)} %wq.1, bf16[4096,256]{1,0:T(8,128)(2,1)} %wk.1, ...), custom_call_target="tpu_custom_call" | custom-call | tf_op jit(solution)/shard_map/pallas_call | solution.py:653
  90.8 1.9 %copy.10 = f32[256,512]{1,0:T(8,128)} copy(f32[256,512]{1,0:T(8,128)} %shard_map.82) | data formatting | bytes 1048576

commit v5 on v4

--- a/solution.py
+++ b/solution.py
@@ -257,9 +257,9 @@
             for copy in t_forward(z - d):
                 copy.start()
 
-        @pl.when(d > 2)
-        def _():
-            source = z - d + 2
+        @pl.when(d > 4)
+        def _():
+            source = z - d + 4
             for copy in t_forward(source):
                 copy.wait()
             for a in range(2):
@@ -267,7 +267,7 @@
 
         return carry
 
-    lax.fori_loop(1, jnp.where(z > 0, z + 3, 1), t_step, 0)
+    lax.fori_loop(1, jnp.where(z > 0, z + 5, 1), t_step, 0)
     for a in range(2):
         prefixes[a, 0] = totals[a]
         prefixes[a, 1] = nn3(totals[a], products[a, 0])

time: 93.4 us -> 92.6 us (level)
  no operation moved by 1% of the time
where the time goes in v5:
time: 92.6 us; the launch traced here: 92.5 us
  Pallas kernels  90.6 us (98%)
  local copies, waits for them, and re-layouts  1.87 us (2%)
    pallas_call x1, Pallas kernels, on_device(): pl.pallas_call(whole_kernel, out_shape=jax.ShapeDtypeStruct(wide, F32), i...  90.6 us
    unnamed x1, local copies, waits for them, and re-layouts  1.87 us

profile of v5, /device:TPU:1, one launch (start us, length us, event | category | flops | bytes accessed | tf_op | source)
XLA Modules:
  0.0 92.5 jit_solution(12685262500400919928)
XLA Ops:
  0.0 90.6 %shard_map.82 = f32[256,512]{1,0:T(8,128)} custom-call(bf16[256,256]{1,0:T(8,128)(2,1)} %hh_in.1, bf16[256,256]{1,0:T(8,128)(2,1)} %q_in.1, bf16[256,256]{1,0:T(8,128)(2,1)} %k_in.1, bf16[256,256]{1,0:T(8,128)(2,1)} %v_in.1, bf16[256,256]{1,0:T(8,128)(2,1)} %c_in.1, bf16[4096,256]{1,0:T(8,128)(2,1)} %wq.1, bf16[4096,256]{1,0:T(8,128)(2,1)} %wk.1, ...), custom_call_target="tpu_custom_call" | custom-call | tf_op jit(solution)/shard_map/pallas_call | solution.py:653
  90.6 1.9 %copy.10 = f32[256,512]{1,0:T(8,128)} copy(f32[256,512]{1,0:T(8,128)} %shard_map.82) | data formatting | bytes 1048576
